TPU v7x, 256 devices: a whole 4x4x8 slice. The times are simulated.
256 devices in a mesh: tm: 64 (over x, y, z_hi, core), grp: 4 (over z_lo).
Axes of the slice: x: 4, y: 4, z: 8 (z_hi: 2, z_lo: 4; z = z_hi * 4 + z_lo), core: 2. Of those that a mesh axis runs over, the one named last changes fastest.
Arguments:
- traces: bfloat16 [4096, 32768], P('grp', 'tm'), may hold values from -6 to 6
- fir_taps: bfloat16 [129], replicated, may hold values from -0.5 to 0.5
- gauge_half: int32 [4096], P('grp'), may hold values from 1 to 8
- sta_length: int32 [4096], P('grp'), may hold values from 8 to 16
- lta_length: int32 [4096], P('grp'), may hold values from 64 to 128
- band_edges: int32 [9], replicated, may hold values from 1 to 127, as said below
Outputs:
- trigger_ratio: bfloat16 [4, 1024, 32768], P('grp', 'tm')
- band_signature: float32 [4, 1024, 8, 128], P('grp', 'tm')
Inputs may be any that keep to these rules, and one draw needn't show every extreme that they name: band_edges rises strictly; its first entry is 1 and its last 127.
All inputs are finite; a program needn't handle non-finite values.
Results may differ from a plain program's by a relative error of at most 0.0036.
Values may be sent and summed in bfloat16 or wider, within the bound.
A program may use at most 64 MiB of HBM per device.

v0:
```python
import math

import jax
import jax.numpy as jnp
from jax import lax
from jax.sharding import PartitionSpec as P

NTAPS = 129
HMAX = 8
SMIN = 8
SMAX = 16
LMIN = 64
LMAX = 128
FRAME = 256
NBANDS = 8


def extended_2(x, sides, width):
    for axis, dim in sides:
        count, length = (lax.axis_size(axis), x.shape[dim])
        up = [(i, (i + 1) % count) for i in range(count - 1)]
        down = [(j, i) for i, j in up]
        last = lax.slice_in_dim(x, length - width, length, axis=dim)
        leading = lax.slice_in_dim(x, 0, width, axis=dim)
        before = lax.ppermute(last, axis, up)
        after = lax.ppermute(leading, axis, down)
        x = jnp.concatenate([before, x, after], axis=dim)
    return x


def gauge_apply(extended, half_gauge):
    count = half_gauge.shape[0]
    centre = extended[HMAX : HMAX + count].astype(jnp.float32)
    sides = jnp.zeros(centre.shape, jnp.float32)
    for offset in range(1, HMAX + 1):
        paired = extended[HMAX + offset : HMAX + offset + count].astype(jnp.float32) + extended[
            HMAX - offset : HMAX - offset + count
        ].astype(jnp.float32)
        sides = jnp.where((half_gauge == offset)[:, None], paired, sides)
    return (centre - 0.5 * sides).astype(jnp.bfloat16)


def toeplitz_taps(fir_taps, block):
    reach = NTAPS - 1
    padded_row = jnp.concatenate([fir_taps, jnp.zeros((block,), fir_taps.dtype)])
    return jnp.tile(padded_row, block)[: block * (block + reach)].reshape(block, block + reach)


def run_filter(padded, toeplitz):
    block = toeplitz.shape[0]
    reach = NTAPS - 1
    count = padded.shape[0]
    blocks = (padded.shape[1] - reach) // block
    leading = padded[:, : blocks * block].reshape(count, blocks, block)
    trailing = jnp.pad(padded[:, block:], ((0, 0), (0, block - reach)))
    trailing = trailing.reshape(count, blocks, block)[:, :, :reach]
    windows = jnp.concatenate([leading, trailing], axis=2)
    result = jnp.einsum("rnk,tk->rnt", windows, toeplitz, preferred_element_type=jnp.float32)
    return result.reshape(count, blocks * block)


def shift_later(values, amount):
    total = values.shape[-1]
    head = jnp.zeros(values.shape[:-1] + (amount,), values.dtype)
    return jnp.concatenate([head, values[..., : total - amount]], axis=-1)


def both_window_sums(energy, sta, lta):
    running = jnp.cumsum(energy, axis=1)
    stacked = jnp.stack([shift_later(running, SMIN), shift_later(running, LMIN)])
    extra = jnp.stack([sta - SMIN, lta - LMIN])
    spread = max(SMAX - SMIN, LMAX - LMIN)
    for digit in range(max(spread, 1).bit_length()):
        moved = shift_later(stacked, 1 << digit)
        chosen = extra >> digit & 1 == 1
        stacked = jnp.where(chosen[:, :, None], moved, stacked)
    return (running - stacked[0], running - stacked[1])


def detect(filtered, sta, lta, edges):
    count, total = filtered.shape
    frames_count = total // FRAME
    half = FRAME // 2
    energy = filtered * filtered
    short_sum, long_sum = both_window_sums(energy, sta, lta)
    short_mean = short_sum / sta.astype(jnp.float32)[:, None]
    long_mean = long_sum / lta.astype(jnp.float32)[:, None]
    ratio = (short_mean / jnp.maximum(long_mean, 0.5)).astype(jnp.bfloat16)
    positions = jnp.arange(FRAME, dtype=jnp.int32)
    bins = jnp.arange(half, dtype=jnp.int32)
    hann_window = 0.5 - 0.5 * jnp.cos(2.0 * math.pi * positions.astype(jnp.float32) / FRAME)
    phase = positions[:, None] * bins[None, :] % FRAME
    angle = 2.0 * math.pi * phase.astype(jnp.float32) / FRAME
    table = jnp.concatenate([jnp.cos(angle), jnp.sin(angle)], axis=1)
    frames = filtered.reshape(count * frames_count, FRAME) * hann_window[None, :]
    spectrum = jnp.dot(
        frames, table, precision=lax.Precision.HIGHEST, preferred_element_type=jnp.float32
    )
    power = spectrum[:, :half] * spectrum[:, :half] + spectrum[:, half:] * spectrum[:, half:]
    lower = edges[:-1]
    upper = edges[1:]
    select = ((bins[:, None] >= lower[None, :]) & (bins[:, None] < upper[None, :])).astype(
        jnp.float32
    )
    widths = (upper - lower).astype(jnp.float32)
    band = (
        jnp.dot(power, select, precision=lax.Precision.HIGHEST, preferred_element_type=jnp.float32)
        / widths[None, :]
    )
    band = band.reshape(count, frames_count, NBANDS).transpose(0, 2, 1)
    return (ratio, jnp.log1p(band / FRAME))


def body(traces, fir_taps, gauge_half, sta_length, lta_length, band_edges):
    slabs = lax.axis_size("tm")
    channels, local_time = traces.shape
    per_device = channels // slabs
    reach = (NTAPS - 1) // 2
    extended = extended_2(traces, (("grp", 0),), HMAX)
    gauged = gauge_apply(extended, gauge_half)
    block = min(local_time, 512)
    toeplitz = toeplitz_taps(fir_taps, block)
    position = lax.axis_index("tm")
    own_sta = lax.dynamic_slice_in_dim(sta_length, position * per_device, per_device)
    own_lta = lax.dynamic_slice_in_dim(lta_length, position * per_device, per_device)
    with_rims = extended_2(gauged, (("tm", 1),), reach)
    filtered = run_filter(with_rims, toeplitz)
    arrived = lax.all_to_all(
        filtered.reshape(slabs, per_device, local_time),
        "tm",
        split_axis=0,
        concat_axis=2,
        tiled=True,
    )
    whole_trace = arrived.reshape(per_device, slabs * local_time)
    ratio, signature = detect(whole_trace, own_sta, own_lta, band_edges)
    return (
        ratio.reshape(1, per_device, ratio.shape[1]),
        signature.reshape(1, per_device, NBANDS, signature.shape[2]),
    )


def solution(mesh):
    in_specs = (P("grp", "tm"), P(), P("grp"), P("grp"), P("grp"), P())
    out_specs = (P("grp", "tm", None), P("grp", "tm", None, None))
    return jax.shard_map(body, mesh=mesh, in_specs=in_specs, out_specs=out_specs, check_vma=False)
```

profile of v0, /device:TPU:33, one launch (start us, length us, event | category | flops | bytes accessed | tf_op | source)
XLA Modules:
  0.0 145.3 jit_solution(14770827310496362707)
XLA Ops:
  1.4 1.9 %collective-permute-start = (bf16[8,512]{1,0:T(8,128)(2,1)S(1)}, bf16[8,512]{1,0:T(8,128)(2,1)S(1)}, u32[]{:S(2)}, u32[]{:S(2)}) collective-permute-start(bf16[8,512]{1,0:T(8,128)(2,1)S(1)} %get-tuple-element.6), channel_id=1, source_target_pairs={{1,0},{2,1},{3,2},{5,4},{6,5},{7,6},{9,8},{10,9},{11,10},{13,12},{... | collective-permute-start | bytes 24584 | tf_op jit(solution)/shard_map/ppermute | solution.py:26
  3.4 3.5 %collective-permute-start.1 = (bf16[8,512]{1,0:T(8,128)(2,1)S(1)}, bf16[8,512]{1,0:T(8,128)(2,1)S(1)}, u32[]{:S(2)}, u32[]{:S(2)}) collective-permute-start(bf16[8,512]{1,0:T(8,128)(2,1)S(1)} %get-tuple-element.7), channel_id=1, source_target_pairs={{0,1},{1,2},{2,3},{4,5},{5,6},{6,7},{8,9},{9,10},{10,11},{12,13},{... | collective-permute-start | bytes 24584 | tf_op jit(solution)/shard_map/ppermute | solution.py:25
  7.8 1.4 constant_dynamic-update-slice_fusion.1
  9.2 4.5 %subtract_convert_fusion = bf16[1024,512]{1,0:T(8,128)(2,1)S(1)} fusion(bf16[1024,512]{1,0:T(8,128)(2,1)S(1)} %copy-done.2, bf16[1032,512]{1,0:T(8,128)(2,1)S(1)} %get-tuple-element.9, bf16[1032,512]{1,0:T(8,128)(2,1)S(1)} %constant_dynamic-update-slice_fusion, pred[1024]{0:T(1024)(128)(4,1)S(1)} %get-tuple-element.20, ...), kind=kLoop, calls=%fused_computation.28 | loop fusion | flops 18874368 | bytes 18882560 | tf_op jit(solution)/shard_map/convert_element_type | solution.py:40
  13.9 10.6 %collective-permute-start.2 = (bf16[1024,64]{1,0:T(8,128)(2,1)S(1)}, bf16[1024,64]{1,0:T(8,128)(2,1)S(1)}, u32[]{:S(2)}, u32[]{:S(2)}) collective-permute-start(bf16[1024,64]{1,0:T(8,128)(2,1)S(1)} %get-tuple-element.4), channel_id=1, source_target_pairs={{0,4},{4,8},{8,12},{12,16},{16,20},{20,24},{24,28},{28,32},{32,36}... | collective-permute-start | bytes 393224 | tf_op jit(solution)/shard_map/ppermute | solution.py:25
  24.5 1.9 %collective-permute-start.3 = (bf16[1024,64]{1,0:T(8,128)(2,1)S(1)}, bf16[1024,64]{1,0:T(8,128)(2,1)S(1)}, u32[]{:S(2)}, u32[]{:S(2)}) collective-permute-start(bf16[1024,64]{1,0:T(8,128)(2,1)S(1)} %get-tuple-element.5), channel_id=1, source_target_pairs={{4,0},{8,4},{12,8},{16,12},{20,16},{24,20},{28,24},{32,28},{36,32}... | collective-permute-start | bytes 393224 | tf_op jit(solution)/shard_map/ppermute | solution.py:26
  28.3 2.3 %collective-permute-done.2 = bf16[1024,64]{1,0:T(8,128)(2,1)S(1)} collective-permute-done((bf16[1024,64]{1,0:T(8,128)(2,1)S(1)}, bf16[1024,64]{1,0:T(8,128)(2,1)S(1)}, u32[]{:S(2)}, u32[]{:S(2)}) %collective-permute-start.2) | collective-permute-done | bytes 131104 | tf_op jit(solution)/shard_map/ppermute | solution.py:25
  30.6 8.3 %collective-permute-done.3 = bf16[1024,64]{1,0:T(8,128)(2,1)S(1)} collective-permute-done((bf16[1024,64]{1,0:T(8,128)(2,1)S(1)}, bf16[1024,64]{1,0:T(8,128)(2,1)S(1)}, u32[]{:S(2)}, u32[]{:S(2)}) %collective-permute-start.3) | collective-permute-done | bytes 131104 | tf_op jit(solution)/shard_map/ppermute | solution.py:26
  39.7 2.4 %fusion.13 = f32[64,16,512]{2,1,0:T(8,128)} fusion(bf16[512,640,1]{1,0,2:T(8,128)(2,1)S(1)} %reshape.237, bf16[64,16,128]{2,1,0:T(8,128)(2,1)S(1)} %bitcast.58, bf16[64,16,512]{2,1,0:T(8,128)(2,1)S(1)} %bitcast.57), kind=kOutput, calls=%fused_computation.30 | convolution fusion | flops 673710080 | bytes 4063232 | tf_op jit(solution)/shard_map/rnk,tk->rnt/dot_general | solution.py:58
  42.1 11.3 %all-to-all-start = ((f32[64,16,512]{2,1,0:T(8,128)}), f32[64,16,512]{2,1,0:T(8,128)S(1)}, u32[]{:S(2)}, u32[]{:S(2)}) async-start(f32[64,16,512]{2,1,0:T(8,128)} %fusion.13), calls=%async_computation | async-start | bytes 4194304 | tf_op jit(solution)/shard_map/all_to_all | solution.py:128
  54.9 54.3 %all-to-all-done = f32[64,16,512]{2,1,0:T(8,128)S(1)} async-done(((f32[64,16,512]{2,1,0:T(8,128)}), f32[64,16,512]{2,1,0:T(8,128)S(1)}, u32[]{:S(2)}, u32[]{:S(2)}) %all-to-all-start) | async-done | bytes 2097184 | tf_op jit(solution)/shard_map/all_to_all | solution.py:128
  109.1 2.5 %copy.15 = f32[1,16,64,512]{3,2,1,0:T(8,128)} copy(f32[1,16,64,512]{3,1,2,0:T(8,128)S(1)} %bitcast.52) | data formatting | bytes 4194304 | tf_op jit(solution)/shard_map/all_to_all | solution.py:128
  111.7 2.7 %reshape_reshape.4 = f32[2048,256]{1,0:T(8,128)} reshape(f32[1,16,64,512]{3,2,1,0:T(8,128)} %copy.15) | data formatting | bytes 4194304 | tf_op jit(solution)/shard_map/reshape;reshape | solution.py:95
  115.9 1.4 mul.65
  117.3 3.2 %copy.10 = f32[16,256,128]{1,0,2:T(8,128)} copy(f32[16,256,128]{2,1,0:T(8,128)} %mul.65) | data formatting | bytes 4194304 | tf_op jit(solution)/shard_map/mul | solution.py:84
  120.4 1.8 %fusion.43 = f32[16,256,128]{1,0,2:T(8,128)S(1)} fusion(f32[16,256,128]{1,0,2:T(8,128)} %copy.10), kind=kOutput, calls=%fused_computation.98 | output fusion | flops 66584576 | bytes 4194304 | tf_op jit(solution)/shard_map/reduce-window
  123.2 1.6 %broadcast_add_fusion = f32[16,256,128]{1,0,2:T(8,128)} fusion(f32[16,256,128]{1,0,2:T(8,128)S(1)} %fusion.43, f32[16,256]{1,0:T(8,128)S(1)} %pad_slice_fusion.2), kind=kLoop, calls=%fused_computation.42 | loop fusion | flops 524288 | bytes 4210688 | tf_op jit(solution)/shard_map/reduce_window_sum
  124.7 2.0 %copy.13 = f32[16,256,128]{2,1,0:T(8,128)S(1)} copy(f32[16,256,128]{1,0,2:T(8,128)} %broadcast_add_fusion) | data formatting | bytes 4194304 | tf_op jit(solution)/shard_map/reduce_window_sum
  126.7 1.5 %reduce_window_sum.36 = f32[1,16,32768]{2,1,0:T(8,128)} reshape(f32[16,256,128]{2,1,0:T(8,128)S(1)} %copy.13) | data formatting | bytes 4194304 | tf_op jit(solution)/shard_map/reduce_window_sum
  132.1 2.2 %pad_select_fusion.5 = f32[2,16,32768]{2,1,0:T(8,128)S(1)} fusion(f32[2,16,32766]{2,1,0:T(8,128)S(1)} %bitcast.56, pred[2,16]{1,0:T(4,128)(4,1)S(1)} %get-tuple-element.27, f32[1,16,32768]{2,1,0:T(8,128)S(1)} %get-tuple-element.32, f32[1,16,32768]{2,1,0:T(8,128)S(1)} %get-tuple-element.33, f32[2,16,32767]{2,1,0:T(8,128)S(1)} %fusion, ...), kind=kLoop, calls=%fused_computation.10 | loop fusion | flops 3145728 | bytes 16776896 | tf_op jit(solution)/shard_map/jit(_where)/select_n | solution.py:76
  138.9 1.4 pad_select_fusion
  140.5 1.9 %fusion.10 = f32[2048,256]{1,0:T(8,128)S(1)} fusion(f32[2048,256]{1,0:T(8,128)S(1)} %copy-done, f32[256]{0:T(256)S(1)} %multiply_subtract_fusion, f32[256,128]{1,0:T(8,128)S(1)} %get-tuple-element.36, f32[256,128]{1,0:T(8,128)S(1)} %get-tuple-element.37), kind=kOutput, calls=%fused_computation.24 | convolution fusion | flops 1611202560 | bytes 4457472 | tf_op jit(solution)/shard_map/dot_general | solution.py:96
  142.4 1.3 fusion.17
  143.7 1.6 %fusion.12 = bf16[1,16,32768]{2,1,0:T(8,128)(2,1)} fusion(f32[1,16,32768]{2,1,0:T(8,128)S(1)} %copy-done.1, f32[2,16,32768]{2,1,0:T(8,128)S(1)} %pad_select_fusion, f32[16]{0:T(128)S(1)} %get-tuple-element.12, f32[16]{0:T(128)S(1)} %get-tuple-element.35), kind=kLoop, calls=%fused_computation.29 | loop fusion | flops 3670016 | bytes 7340160 | tf_op jit(solution)/shard_map/convert_element_type | solution.py:88
  (48 shorter events, 16.9 us)
Async XLA Ops:
  0.6 8.5 %copy-start.2 = (bf16[1024,512]{1,0:T(8,128)(2,1)S(1)}, bf16[1024,512]{1,0:T(8,128)(2,1)}, u32[]{:S(2)}) copy-start(bf16[1024,512]{1,0:T(8,128)(2,1)} %param.6) | copy-start | bytes 3145732
  1.4 7.7 %collective-permute-start = (bf16[8,512]{1,0:T(8,128)(2,1)S(1)}, bf16[8,512]{1,0:T(8,128)(2,1)S(1)}, u32[]{:S(2)}, u32[]{:S(2)}) collective-permute-start(bf16[8,512]{1,0:T(8,128)(2,1)S(1)} %get-tuple-element.6), channel_id=1, source_target_pairs={{1,0},{2,1},{3,2},{5,4},{6,5},{7,6},{9,8},{10,9},{11,10},{13,12},{... | collective-permute-start | bytes 24584 | tf_op jit(solution)/shard_map/ppermute | solution.py:26
  3.4 4.4 %collective-permute-start.1 = (bf16[8,512]{1,0:T(8,128)(2,1)S(1)}, bf16[8,512]{1,0:T(8,128)(2,1)S(1)}, u32[]{:S(2)}, u32[]{:S(2)}) collective-permute-start(bf16[8,512]{1,0:T(8,128)(2,1)S(1)} %get-tuple-element.7), channel_id=1, source_target_pairs={{0,1},{1,2},{2,3},{4,5},{5,6},{6,7},{8,9},{9,10},{10,11},{12,13},{... | collective-permute-start | bytes 24584 | tf_op jit(solution)/shard_map/ppermute | solution.py:25
  9.2 17.2 %copy-start.4 = (bf16[129]{0:T(256)(128)(2,1)S(1)}, bf16[129]{0:T(256)(128)(2,1)}, u32[]{:S(2)}) copy-start(bf16[129]{0:T(256)(128)(2,1)} %param.7) | copy-start | bytes 778
  13.9 16.7 %collective-permute-start.2 = (bf16[1024,64]{1,0:T(8,128)(2,1)S(1)}, bf16[1024,64]{1,0:T(8,128)(2,1)S(1)}, u32[]{:S(2)}, u32[]{:S(2)}) collective-permute-start(bf16[1024,64]{1,0:T(8,128)(2,1)S(1)} %get-tuple-element.4), channel_id=1, source_target_pairs={{0,4},{4,8},{8,12},{12,16},{16,20},{20,24},{24,28},{28,32},{32,36}... | collective-permute-start | bytes 393224 | tf_op jit(solution)/shard_map/ppermute | solution.py:25
  24.5 14.4 %collective-permute-start.3 = (bf16[1024,64]{1,0:T(8,128)(2,1)S(1)}, bf16[1024,64]{1,0:T(8,128)(2,1)S(1)}, u32[]{:S(2)}, u32[]{:S(2)}) collective-permute-start(bf16[1024,64]{1,0:T(8,128)(2,1)S(1)} %get-tuple-element.5), channel_id=1, source_target_pairs={{4,0},{8,4},{12,8},{16,12},{20,16},{24,20},{28,24},{32,28},{36,32}... | collective-permute-start | bytes 393224 | tf_op jit(solution)/shard_map/ppermute | solution.py:26
  42.1 12.7 %copy-start.3 = (s32[9]{0:T(128)S(1)}, s32[9]{0:T(128)}, u32[]{:S(2)}) copy-start(s32[9]{0:T(128)} %param.11) | copy-start | bytes 112
  42.1 67.0 %all-to-all-start = ((f32[64,16,512]{2,1,0:T(8,128)}), f32[64,16,512]{2,1,0:T(8,128)S(1)}, u32[]{:S(2)}, u32[]{:S(2)}) async-start(f32[64,16,512]{2,1,0:T(8,128)} %fusion.13), calls=%async_computation | async-start | bytes 4194304 | tf_op jit(solution)/shard_map/all_to_all | solution.py:128
  138.9 1.6 %copy-start = (f32[2048,256]{1,0:T(8,128)S(1)}, f32[2048,256]{1,0:T(8,128)}, u32[]{:S(2)}) copy-start(f32[2048,256]{1,0:T(8,128)} %reshape_reshape.4) | copy-start | bytes 6291460
  140.5 3.2 %copy-start.1 = (f32[1,16,32768]{2,1,0:T(8,128)S(1)}, f32[1,16,32768]{2,1,0:T(8,128)}, u32[]{:S(2)}) copy-start(f32[1,16,32768]{2,1,0:T(8,128)} %reduce_window_sum.36) | copy-start | bytes 6291460
where the time goes:
time: 146 us; the launch traced here: 145 us
  waiting for transfers between devices  65 us (45%)
  starting transfers between devices  29.3 us (20%)
  other arithmetic  22.9 us (16%)
  local copies, waits for them, and re-layouts  21.6 us (15%)
  matrix products  5.55 us (4%)
    all_to_all x1, waiting for transfers between devices, body(): lax.all_to_all(filtered.reshape(slabs, per_device, local_time), 'tm', spl...  54.3 us
    ppermute x2, starting transfers between devices, extended_2(): before = lax.ppermute(last, axis, up)  14.2 us
    all_to_all x1, starting transfers between devices, body(): lax.all_to_all(filtered.reshape(slabs, per_device, local_time), 'tm', spl...  11.3 us
    select_n x7, other arithmetic, both_window_sums(): stacked = jnp.where(chosen[:, :, None], moved, stacked)  9.35 us
    ppermute x2, waiting for transfers between devices, extended_2(): after = lax.ppermute(leading, axis, down)  8.31 us
    mul x3, local copies, waits for them, and re-layouts, detect(): energy = filtered * filtered  5.78 us
    convert_element_type x1, other arithmetic, gauge_apply(): return (centre - 0.5 * sides).astype(jnp.bfloat16)  4.53 us
    another operation x5, other arithmetic  4.03 us
  transfers between devices with their start and end apart: 5, of which 4 were waited for; matrix products, arithmetic and copies ran while one was open for 4% of the time, Pallas kernels for 0%

commit v1 on v0

v1 whole, which is shorter than its diff:
```python
import functools
import math

import jax
import jax.numpy as jnp
import numpy as np
from jax import lax
from jax.experimental import pallas as pl
from jax.experimental.pallas import tpu as pltpu
from jax.sharding import PartitionSpec as P

NTAPS = 129
REACH = 64
LANES = 128
FRAME = 256
NBANDS = 8
ROWS = 16
MESH = pl.DeviceIdType.MESH
F32 = jnp.float32
BF16 = jnp.bfloat16


def spectral_tables():
    n = np.arange(FRAME)
    k = np.arange(FRAME // 2)
    angle = 2.0 * math.pi * ((n[:, None] * k[None, :]) % FRAME) / FRAME
    hann = 0.5 - 0.5 * np.cos(2.0 * math.pi * n / FRAME)
    table = np.concatenate([np.cos(angle), np.sin(angle)], axis=1) * hann[:, None]
    high = table.astype(jnp.bfloat16)
    low = (table - high.astype(np.float64)).astype(jnp.bfloat16)
    return high, low


def iota(shape, dim):
    return lax.broadcasted_iota(jnp.int32, shape, dim)


def split(x):
    high = x.astype(BF16)
    return high, (x - high.astype(F32)).astype(BF16)


def dot(a, b):
    return jnp.dot(a, b, preferred_element_type=F32)


def dot_nt(a, b):
    return lax.dot_general(a, b, (((1,), (1,)), ((), ())), preferred_element_type=F32)


def gauge_matrix(half, width, off):
    n = half.shape[0]
    if width > LANES:
        half = jnp.concatenate([half] * (width // LANES), axis=1)
    rel = (iota((n, width), 1) - iota((n, width), 0) - off).astype(F32)
    side = jnp.where(jnp.abs(rel) == half, -0.5, 0.0)
    return jnp.where(rel == 0.0, 1.0, side).astype(BF16)


def kernel(
    slabs, groups,
    traces, taps, half, sta, lta, edges, th, tl,
    ratio_out, sig_out,
    x, ga, r, lo_halo, hi_halo, toep, windows, sel, widths, fa, fb, ra, rb,
    in_sem, send_sem, recv_sem, hsend, hrecv,
):
    me = lax.axis_index("tm")
    g = lax.axis_index("grp")
    chans = x.shape[0]
    block = min(LANES, chans)
    per = block // ROWS
    has_lo = g > 0
    has_hi = g < groups - 1

    load = pltpu.make_async_copy(traces, x, in_sem)
    load.start()
    barrier = pltpu.get_barrier_semaphore()

    @pl.loop(1, slabs)
    def _(k):
        pl.semaphore_signal(barrier, inc=1, device_id=((me + k) % slabs, g), device_id_type=MESH)

    @pl.when(has_lo)
    def _():
        pl.semaphore_signal(barrier, inc=1, device_id=(me, g - 1), device_id_type=MESH)

    @pl.when(has_hi)
    def _():
        pl.semaphore_signal(barrier, inc=1, device_id=(me, g + 1), device_id_type=MESH)

    def half_column(i):
        row = jnp.broadcast_to(half[pl.ds(i, 1), :], (LANES, LANES))
        return row.T[:block]

    load.wait()
    width = min(2 * LANES, chans)

    @pl.loop(0, chans // block)
    def _(i):
        start = jnp.clip(i * block - REACH, 0, chans - width)
        rows = x[pl.ds(pl.multiple_of(start, ROWS), width), :]
        m = gauge_matrix(half_column(i), width, i * block - start)
        ga[pl.ds(i * per, per)] = dot(m, rows).astype(BF16).reshape(per, ROWS, x.shape[1])

    neighbours = jnp.where(has_lo, 1, 0) + jnp.where(has_hi, 1, 0)
    pl.semaphore_wait(barrier, slabs - 1 + neighbours)

    def to_hi():
        return pltpu.make_async_remote_copy(
            src_ref=traces.at[pl.ds(chans - ROWS, ROWS)], dst_ref=lo_halo, send_sem=hsend.at[0],
            recv_sem=hrecv.at[0], device_id=(me, g + 1), device_id_type=MESH)

    def to_lo():
        return pltpu.make_async_remote_copy(
            src_ref=traces.at[pl.ds(0, ROWS)], dst_ref=hi_halo, send_sem=hsend.at[1],
            recv_sem=hrecv.at[1], device_id=(me, g - 1), device_id_type=MESH)

    @pl.when(has_hi)
    def _():
        to_hi().start()

    @pl.when(has_lo)
    def _():
        to_lo().start()

    def send(d):
        return pltpu.make_async_remote_copy(
            src_ref=ga.at[d], dst_ref=r.at[me + 1], send_sem=send_sem.at[d],
            recv_sem=recv_sem.at[me], device_id=(d, g), device_id_type=MESH)

    early = min(16, slabs)

    @pl.loop(1, early)
    def _(k):
        d = (me + k) % slabs

        @pl.when(jnp.logical_and(d != 0, d != slabs - 1))
        def _():
            send(d).start()

    @pl.when(has_lo)
    def _():
        to_hi().wait_recv()

    @pl.when(jnp.logical_not(has_lo))
    def _():
        lo_halo[...] = jnp.zeros_like(lo_halo)

    @pl.when(has_hi)
    def _():
        to_lo().wait_recv()

    @pl.when(jnp.logical_not(has_hi))
    def _():
        hi_halo[...] = jnp.zeros_like(hi_halo)

    edge = min(LANES - ROWS, chans)
    first = jnp.concatenate([lo_halo[...], x[0:edge, :]], axis=0)
    m = gauge_matrix(half_column(0)[:ROWS], LANES, ROWS)[:, : edge + ROWS]
    ga[0] = dot(m, first).astype(BF16)
    last = jnp.concatenate([x[chans - edge :, :], hi_halo[...]], axis=0)
    m = gauge_matrix(half_column(chans // block - 1)[block - ROWS :], LANES, edge - ROWS)[:, : edge + ROWS]
    ga[slabs - 1] = dot(m, last).astype(BF16)

    @pl.loop(1, slabs)
    def _(k):
        d = (me + k) % slabs

        @pl.when(jnp.logical_or(k >= early, jnp.logical_or(d == 0, d == slabs - 1)))
        def _():
            send(d).start()

    r[pl.ds(me + 1, 1)] = ga[pl.ds(me, 1)]
    r[0] = jnp.zeros(r.shape[1:], BF16)
    r[slabs + 1] = jnp.zeros(r.shape[1:], BF16)
    zero = jnp.zeros((2 * ROWS, LANES), F32)
    fa[0 : 2 * ROWS] = zero
    fb[0 : 2 * ROWS] = zero
    row = jnp.broadcast_to(taps[...], (FRAME, 2 * FRAME))
    toep[...] = pltpu.roll(row, 0, 1, stride=1, stride_axis=0).astype(BF16)
    bands = iota((ROWS, LANES), 0)
    lower = jnp.zeros((ROWS, LANES), jnp.int32)
    upper = jnp.zeros((ROWS, LANES), jnp.int32)
    for b in range(NBANDS):
        lower = jnp.where(bands == b, edges[b], lower)
        upper = jnp.where(bands == b, edges[b + 1], upper)
    bins = iota((ROWS, LANES), 1)
    sel[...] = jnp.where(jnp.logical_and(bins >= lower, bins < upper), 1.0, 0.0).astype(BF16)
    widths[...] = (upper - lower).astype(F32)[:NBANDS]

    @pl.loop(0, ROWS)
    def _(c):
        back = iota((FRAME, LANES), 1) + LANES - iota((FRAME, LANES), 0)
        past = back >= 0
        short = jnp.where(jnp.logical_and(past, back < sta[me * ROWS + c]), 1.0, 0.0).astype(BF16)
        long = jnp.where(jnp.logical_and(past, back < lta[me * ROWS + c]), 1.0, 0.0).astype(BF16)
        windows[c] = jnp.concatenate([short, long], axis=1)

    @pl.loop(1, slabs)
    def _(k):
        s = (me + k) % slabs
        pltpu.make_async_remote_copy(
            src_ref=ga.at[s], dst_ref=r.at[s + 1], send_sem=send_sem.at[s],
            recv_sem=recv_sem.at[s], device_id=(s, g), device_id_type=MESH).wait_recv()

    step = min(8, slabs)
    rows = step * ROWS

    @pl.loop(0, slabs // step)
    def _(i):
        s0 = i * step

        def tile(slab, q):
            return r[pl.ds(s0 + slab, step), :, q * LANES : (q + 1) * LANES].reshape(rows, LANES)

        own = [tile(1, q) for q in range(4)]
        for f, parts in enumerate(([tile(0, 3)] + own[:3], own[1:] + [tile(2, 0)])):
            out = dot_nt(jnp.concatenate(parts, axis=1), toep[...])
            for j in range(step):
                at = pl.multiple_of(((s0 + 1 + j) * 2 + f) * ROWS, ROWS)
                fa[pl.ds(at, ROWS), :] = out[j * ROWS : (j + 1) * ROWS, :LANES]
                fb[pl.ds(at, ROWS), :] = out[j * ROWS : (j + 1) * ROWS, LANES:]

    frames = 2 * slabs

    @pl.loop(0, ROWS)
    def _(c):
        first = fa[pl.ds(2 * ROWS + c, frames, stride=ROWS), :]
        second = fb[pl.ds(2 * ROWS + c, frames, stride=ROWS), :]
        before = fb[pl.ds(ROWS + c, frames, stride=ROWS), :]
        high, low = split(jnp.concatenate([first, second], axis=1))
        spectrum = dot(high, th[...]) + (dot(low, th[...]) + dot(high, tl[...]))
        power = spectrum[:, :LANES] * spectrum[:, :LANES] + spectrum[:, LANES:] * spectrum[:, LANES:]
        high, low = split(power)
        band = (dot_nt(sel[...], high) + dot_nt(sel[...], low))[:NBANDS]
        sig_out[c] = jnp.log1p(band / widths[:, :frames] / FRAME)
        e0 = jnp.concatenate([before * before, first * first], axis=1)
        e1 = jnp.concatenate([first * first, second * second], axis=1)
        high, low = split(jnp.concatenate([e0, e1], axis=0))
        sums = dot(high, windows[c]) + dot(low, windows[c])
        count_s = jnp.full((1, LANES), sta[me * ROWS + c].astype(F32), F32)
        count_l = jnp.full((1, LANES), lta[me * ROWS + c].astype(F32), F32)
        ratio = (sums[:, :LANES] * (1.0 / count_s)) / jnp.maximum(sums[:, LANES:] * (1.0 / count_l), 0.5)
        ra[pl.ds(c, frames, stride=ROWS), :] = ratio[:frames]
        rb[pl.ds(c, frames, stride=ROWS), :] = ratio[frames:]

    @pl.loop(0, frames)
    def _(f):
        for h, ref in enumerate((ra, rb)):
            at = pl.multiple_of(f * FRAME + h * LANES, LANES)
            ratio_out[:, pl.ds(at, LANES)] = ref[pl.ds(pl.multiple_of(f * ROWS, ROWS), ROWS), :].astype(BF16)

    @pl.when(has_hi)
    def _():
        to_hi().wait_send()

    @pl.when(has_lo)
    def _():
        to_lo().wait_send()

    @pl.loop(1, slabs)
    def _(k):
        send((me + k) % slabs).wait_send()


def body(traces, fir_taps, gauge_half, sta_length, lta_length, band_edges):
    slabs, groups = lax.axis_size("tm"), lax.axis_size("grp")
    chans, local = traces.shape
    taps = jnp.pad(fir_taps.astype(F32), (REACH, 2 * FRAME - REACH - NTAPS))[None, :]
    half = gauge_half.astype(F32)
    half = (jnp.pad(half, (0, -chans % LANES))).reshape(-1, LANES)
    th, tl = (jnp.asarray(t) for t in spectral_tables())
    total = slabs * local
    vmem = pl.BlockSpec(memory_space=pltpu.VMEM)
    smem = pl.BlockSpec(memory_space=pltpu.SMEM)
    padded = (slabs + 1) * 2 * ROWS
    ratio, signature = pl.pallas_call(
        functools.partial(kernel, slabs, groups),
        out_shape=(
            jax.ShapeDtypeStruct((ROWS, total), BF16),
            jax.ShapeDtypeStruct((ROWS, NBANDS, total // FRAME), F32),
        ),
        in_specs=[pl.BlockSpec(memory_space=pl.ANY), vmem, vmem, smem, smem, smem, vmem, vmem],
        out_specs=(vmem, vmem),
        scratch_shapes=[
            pltpu.VMEM((chans, local), BF16),
            pltpu.VMEM((slabs, ROWS, local), BF16),
            pltpu.VMEM((slabs + 2, ROWS, local), BF16),
            pltpu.VMEM((ROWS, local), BF16),
            pltpu.VMEM((ROWS, local), BF16),
            pltpu.VMEM((FRAME, 2 * FRAME), BF16),
            pltpu.VMEM((ROWS, FRAME, FRAME), BF16),
            pltpu.VMEM((ROWS, LANES), BF16),
            pltpu.VMEM((NBANDS, LANES), F32),
            pltpu.VMEM((padded, LANES), F32),
            pltpu.VMEM((padded, LANES), F32),
            pltpu.VMEM((2 * slabs * ROWS, LANES), F32),
            pltpu.VMEM((2 * slabs * ROWS, LANES), F32),
            pltpu.SemaphoreType.DMA,
            pltpu.SemaphoreType.DMA((slabs,)),
            pltpu.SemaphoreType.DMA((slabs,)),
            pltpu.SemaphoreType.DMA((2,)),
            pltpu.SemaphoreType.DMA((2,)),
        ],
        compiler_params=pltpu.CompilerParams(
            collective_id=0, has_side_effects=True, vmem_limit_bytes=48 * 2**20
        ),
        cost_estimate=pl.CostEstimate(flops=4 * 10**9, bytes_accessed=3 * 2**20, transcendentals=0),
    )(traces, taps, half, sta_length, lta_length, band_edges, th, tl)
    return ratio[None], signature[None]


def solution(mesh):
    in_specs = (P("grp", "tm"), P(), P("grp"), P("grp"), P("grp"), P())
    out_specs = (P("grp", "tm", None), P("grp", "tm", None, None))
    return jax.shard_map(body, mesh=mesh, in_specs=in_specs, out_specs=out_specs, check_vma=False)
```

time: 146 us -> 59 us (0.40)
  waiting for transfers between devices: 65 us -> 0 us
  Pallas kernels: 0 us -> 52 us
  starting transfers between devices: 29.3 us -> 0 us
  other arithmetic: 22.9 us -> 1.46 us
  local copies, waits for them, and re-layouts: 21.6 us -> 4.64 us
  matrix products: 5.55 us -> 0 us
    all_to_all x1 -> x0, waiting for transfers between devices: 54.3 us -> none  [body(): lax.all_to_all(filtered.reshape(slabs, per_device, local_time), 'tm', spl...]
    pallas_call x0 -> x1, Pallas kernels: none -> 52 us  [body(): pl.pallas_call(functools.partial(kernel, slabs, groups), out_shape=(jax.S...]
    ppermute x4 -> x0, starting transfers between devices: 18 us -> none  [the longest x2 14.2 us: extended_2(): before = lax.ppermute(last, axis, up)]
    all_to_all x1 -> x0, starting transfers between devices: 11.3 us -> none  [body(): lax.all_to_all(filtered.reshape(slabs, per_device, local_time), 'tm', spl...]
    ppermute x4 -> x0, waiting for transfers between devices: 10.7 us -> none  [the longest x2 8.31 us: extended_2(): after = lax.ppermute(leading, axis, down)]
    select_n x7 -> x0, other arithmetic: 9.35 us -> none  [both_window_sums(): stacked = jnp.where(chosen[:, :, None], moved, stacked)]
    another operation x11 -> x0, local copies, waits for them, and re-layouts: 8.98 us -> none
    convert_element_type x3 -> x0, other arithmetic: 6.88 us -> none  [the longest x1 4.53 us: gauge_apply(): return (centre - 0.5 * sides).astype(jnp.bfloat16)]
  transfers between devices with their start and end apart: 5 -> 0, of which waited for: 4 -> 0; matrix products, arithmetic and copies ran while one was open for 4% -> 0% of each run, Pallas kernels for 0% -> 0%
where the time goes in v1:
time: 59 us; the launch traced here: 58.8 us
  Pallas kernels  52 us (88%)
  local copies, waits for them, and re-layouts  4.64 us (8%)
  other arithmetic  1.46 us (2%)
  between operations  0.65 us (1%)
    pallas_call x1, Pallas kernels, body(): pl.pallas_call(functools.partial(kernel, slabs, groups), out_shape=(jax.S...  52 us
    unnamed x14, local copies, waits for them, and re-layouts  4.64 us

profile of v1, /device:TPU:33, one launch (start us, length us, event | category | flops | bytes accessed | tf_op | source)
XLA Modules:
  0.0 58.8 jit_solution(15645977814574279119)
XLA Ops:
  0.6 0.7 %pad_convert_fusion = f32[512]{0:T(512)S(1)} fusion(bf16[129]{0:T(256)(128)(2,1)} %param.9), kind=kLoop, calls=%fused_computation.1 | loop fusion | flops 512 | bytes 2306 | tf_op jit(solution)/shard_map/broadcast_in_dim | solution.py:269
  1.4 0.0 copy-start.3
  1.4 0.0 copy-start.1
  1.4 0.0 copy-start.2
  1.4 0.7 %convert_bitcast_fusion.half = f32[8,128]{1,0:T(8,128)S(1)} fusion(s32[1024]{0:T(1024)} %param.10), kind=kLoop, calls=%fused_computation | loop fusion | flops 1024 | bytes 8192 | tf_op jit(solution)/shard_map/reshape | solution.py:271
  2.1 0.0 copy-done.3
  2.1 0.0 copy-done.1
  2.1 0.0 copy-done.2
  2.1 0.0 copy-start
  2.1 1.2 %copy-done = bf16[1024,512]{1,0:T(8,128)(2,1)S(1)} copy-done((bf16[1024,512]{1,0:T(8,128)(2,1)S(1)}, bf16[1024,512]{1,0:T(8,128)(2,1)}, u32[]{:S(2)}) %copy-start) | copy-done | bytes 1048600
  3.3 0.0 copy-start.4
  3.3 0.9 %copy-done.4 = bf16[256,256]{1,0:T(8,128)(2,1)S(1)} copy-done((bf16[256,256]{1,0:T(8,128)(2,1)S(1)}, bf16[256,256]{1,0:T(8,128)(2,1)}, u32[]{:S(2)}) %copy-start.4) | copy-done | bytes 131096
  4.2 0.0 copy-start.5
  4.2 0.9 %copy-done.5 = bf16[256,256]{1,0:T(8,128)(2,1)S(1)} copy-done((bf16[256,256]{1,0:T(8,128)(2,1)S(1)}, bf16[256,256]{1,0:T(8,128)(2,1)}, u32[]{:S(2)}) %copy-start.5) | copy-done | bytes 131096
  5.1 52.0 %shard_map.95 = (bf16[16,32768]{1,0:T(8,128)(2,1)S(1)}, f32[16,8,128]{2,1,0:T(8,128)S(1)}) custom-call(bf16[1024,512]{1,0:T(8,128)(2,1)S(1)} %copy-done, f32[1,512]{1,0:T(1,128)S(1)} %bitcast.7, f32[8,128]{1,0:T(8,128)S(1)} %convert_bitcast_fusion.half, s32[1024]{0:T(1024)S(1)} %copy-done.1, s32[1024]{0:T(1024)S(1)} %copy-done.2, s32[9]{0:T(128)S(1)} %copy-done.3, ...), custom_call_target="tpu_custom_call" | custom-call | flops 4000000000 | bytes 3145728 | tf_op jit(solution)/shard_map/pallas_call | solution.py:277
  57.2 1.0 %copy.12 = bf16[1,16,32768]{2,1,0:T(8,128)(2,1)} copy(bf16[1,16,32768]{2,1,0:T(8,128)(2,1)S(1)} %bitcast.5) | data formatting | bytes 2097152
  58.1 0.6 %copy.13 = f32[1,16,8,128]{3,2,1,0:T(8,128)} copy(f32[1,16,8,128]{3,2,1,0:T(8,128)S(1)} %bitcast.6) | data formatting | bytes 131072
Async XLA Ops:
  1.4 0.7 %copy-start.3 = (s32[9]{0:T(128)S(1)}, s32[9]{0:T(128)}, u32[]{:S(2)}) copy-start(s32[9]{0:T(128)} %edges.1) | copy-start | bytes 112
  1.4 0.7 %copy-start.1 = (s32[1024]{0:T(1024)S(1)}, s32[1024]{0:T(1024)}, u32[]{:S(2)}) copy-start(s32[1024]{0:T(1024)} %sta.1) | copy-start | bytes 12292
  1.4 0.7 %copy-start.2 = (s32[1024]{0:T(1024)S(1)}, s32[1024]{0:T(1024)}, u32[]{:S(2)}) copy-start(s32[1024]{0:T(1024)} %lta.1) | copy-start | bytes 12292
  2.1 1.2 %copy-start = (bf16[1024,512]{1,0:T(8,128)(2,1)S(1)}, bf16[1024,512]{1,0:T(8,128)(2,1)}, u32[]{:S(2)}) copy-start(bf16[1024,512]{1,0:T(8,128)(2,1)} %traces.1) | copy-start | bytes 3145732
  3.3 0.9 %copy-start.4 = (bf16[256,256]{1,0:T(8,128)(2,1)S(1)}, bf16[256,256]{1,0:T(8,128)(2,1)}, u32[]{:S(2)}) copy-start(bf16[256,256]{1,0:T(8,128)(2,1)} %constant.9.clone.tl) | copy-start | bytes 393220
  4.2 0.9 %copy-start.5 = (bf16[256,256]{1,0:T(8,128)(2,1)S(1)}, bf16[256,256]{1,0:T(8,128)(2,1)}, u32[]{:S(2)}) copy-start(bf16[256,256]{1,0:T(8,128)(2,1)} %constant.8.clone.th) | copy-start | bytes 393220

commit v2 on v1

v2 whole, which is shorter than its diff:
```python
import functools
import math

import jax
import jax.numpy as jnp
import numpy as np
from jax import lax
from jax.experimental import pallas as pl
from jax.experimental.pallas import tpu as pltpu
from jax.sharding import PartitionSpec as P

NTAPS = 129
REACH = 64
LANES = 128
FRAME = 256
NBANDS = 8
ROWS = 16
STEP = 8
MESH = pl.DeviceIdType.MESH
F32 = jnp.float32
BF16 = jnp.bfloat16


def spectral_table():
    n = np.arange(FRAME)
    k = np.arange(FRAME // 2)
    angle = 2.0 * math.pi * ((n[:, None] * k[None, :]) % FRAME) / FRAME
    hann = 0.5 - 0.5 * np.cos(2.0 * math.pi * n / FRAME)
    table = np.concatenate([np.cos(angle), np.sin(angle)], axis=1) * hann[:, None]
    high = table.astype(jnp.bfloat16)
    low = (table - high.astype(np.float64)).astype(jnp.bfloat16)
    return np.concatenate([high, high, low], axis=0)


def iota(shape, dim):
    return lax.broadcasted_iota(jnp.int32, shape, dim)


def split(x, terms):
    parts = []
    for _ in range(terms - 1):
        parts.append(x.astype(BF16))
        x = x - parts[-1].astype(F32)
    return parts + [x.astype(BF16)]


def dot(a, b):
    return jnp.dot(a, b, preferred_element_type=F32)


def lanes(*parts):
    return jnp.concatenate(parts, axis=1)


def stack(*parts):
    return jnp.concatenate(parts, axis=0)


def gauge_matrix(half, width, off):
    n = half.shape[0]
    if width > LANES:
        half = lanes(*[half] * (width // LANES))
    rel = (iota((n, width), 1) - iota((n, width), 0) - off).astype(F32)
    side = jnp.where(jnp.abs(rel) == half, -0.5, 0.0)
    return jnp.where(rel == 0.0, 1.0, side).astype(BF16)


def kernel(
    slabs, groups,
    traces, taps_in, half_in, sta_in, lta_in, edges_in, table_in,
    ratio_out, sig_out,
    x, ga, r, lo_halo, hi_halo, taps, half, table, toep, sums, sel, widths, turn, scale, bands,
    sta, lta, edges,
    in_sem, send_sem, recv_sem, hsend, hrecv,
):
    me = lax.axis_index("tm")
    g = lax.axis_index("grp")
    chans = x.shape[0]
    block = LANES
    per = block // ROWS
    columns = slabs // 4
    own = me // 4
    has_lo = g > 0
    has_hi = g < groups - 1

    pairs = [(traces, x), (half_in, half), (table_in, table), (taps_in, taps), (sta_in, sta), (lta_in, lta), (edges_in, edges)]
    loads = [pltpu.make_async_copy(a, b, in_sem.at[i]) for i, (a, b) in enumerate(pairs)]
    for load in loads:
        load.start()
    barrier = pltpu.get_barrier_semaphore()

    @pl.loop(1, slabs)
    def _(k):
        pl.semaphore_signal(barrier, inc=1, device_id=((me + k) % slabs, g), device_id_type=MESH)

    @pl.when(has_lo)
    def _():
        pl.semaphore_signal(barrier, inc=1, device_id=(me, g - 1), device_id_type=MESH)

    @pl.when(has_hi)
    def _():
        pl.semaphore_signal(barrier, inc=1, device_id=(me, g + 1), device_id_type=MESH)

    def half_column(i):
        row = jnp.broadcast_to(half[pl.ds(i, 1), :].astype(F32), (LANES, LANES))
        return row.T

    loads[0].wait()
    loads[1].wait()
    width = min(2 * LANES, chans)

    @pl.loop(0, chans // block)
    def _(i):
        start = jnp.clip(i * block - REACH, 0, chans - width)
        rows = x[pl.ds(pl.multiple_of(start, ROWS), width), :]
        m = gauge_matrix(half_column(i), width, i * block - start)
        ga[pl.ds(i * per, per)] = dot(m, rows).astype(BF16).reshape(per, ROWS, x.shape[1])

    neighbours = jnp.where(has_lo, 1, 0) + jnp.where(has_hi, 1, 0)
    pl.semaphore_wait(barrier, slabs - 1 + neighbours)

    def to_hi():
        return pltpu.make_async_remote_copy(
            src_ref=traces.at[pl.ds(chans - ROWS, ROWS)], dst_ref=lo_halo, send_sem=hsend.at[0],
            recv_sem=hrecv.at[0], device_id=(me, g + 1), device_id_type=MESH)

    def to_lo():
        return pltpu.make_async_remote_copy(
            src_ref=traces.at[pl.ds(0, ROWS)], dst_ref=hi_halo, send_sem=hsend.at[1],
            recv_sem=hrecv.at[1], device_id=(me, g - 1), device_id_type=MESH)

    @pl.when(has_hi)
    def _():
        to_hi().start()

    @pl.when(has_lo)
    def _():
        to_lo().start()

    def send(d):
        return pltpu.make_async_remote_copy(
            src_ref=ga.at[d], dst_ref=r.at[me + 1], send_sem=send_sem.at[d],
            recv_sem=recv_sem.at[me], device_id=(d, g), device_id_type=MESH)

    def target(k, e):
        flip = (me // 2 % 2 + 1 + e // 2) % 2
        return (own + columns - k) % columns * 4 + flip * 2 + e % 2

    early = columns // 2

    @pl.loop(0, early * 4)
    def _(i):
        d = target(i // 4, i % 4)

        @pl.when(jnp.logical_and(d != me, jnp.logical_and(d != 0, d != slabs - 1)))
        def _():
            send(d).start()

    @pl.when(has_lo)
    def _():
        to_hi().wait_recv()

    @pl.when(jnp.logical_not(has_lo))
    def _():
        lo_halo[...] = jnp.zeros_like(lo_halo)

    @pl.when(has_hi)
    def _():
        to_lo().wait_recv()

    @pl.when(jnp.logical_not(has_hi))
    def _():
        hi_halo[...] = jnp.zeros_like(hi_halo)

    edge = LANES - ROWS
    m = gauge_matrix(half_column(0)[:ROWS], LANES, ROWS)
    ga[0] = dot(m, stack(lo_halo[...], x[0:edge, :])).astype(BF16)
    m = gauge_matrix(half_column(chans // block - 1)[block - ROWS :], LANES, edge - ROWS)
    ga[slabs - 1] = dot(m, stack(x[chans - edge :, :], hi_halo[...])).astype(BF16)

    @pl.loop(0, columns * 4)
    def _(i):
        d = target(i // 4, i % 4)
        edge_row = jnp.logical_or(d == 0, d == slabs - 1)

        @pl.when(jnp.logical_and(d != me, jnp.logical_or(i >= early * 4, edge_row)))
        def _():
            send(d).start()

    r[pl.ds(me + 1, 1)] = ga[pl.ds(me, 1)]
    r[0] = jnp.zeros(r.shape[1:], BF16)
    r[slabs + 1] = jnp.zeros(r.shape[1:], BF16)
    for load in loads[2:]:
        load.wait()
    row = jnp.broadcast_to(taps[...], (FRAME, 2 * FRAME))
    toep[...] = pltpu.roll(row, 0, 1, stride=1, stride_axis=0).T.astype(BF16)
    earlier = iota((FRAME, 2 * FRAME), 0)
    sample = iota((FRAME, 2 * FRAME), 1)
    tile = sample // LANES % 2 == earlier // LANES
    through = earlier % LANES <= sample % LANES
    upto = jnp.where(jnp.logical_and(tile, through), 1.0, 0.0)
    after = jnp.where(jnp.logical_and(tile, jnp.logical_not(through)), -1.0, 0.0)
    both = jnp.where(sample < FRAME, upto, after).astype(BF16)
    for i in range(3):
        sums[i * FRAME : (i + 1) * FRAME] = both
    bins = iota((LANES, LANES), 0)
    band = iota((LANES, LANES), 1)
    select = jnp.zeros((LANES, LANES), F32)
    width_of = jnp.ones((NBANDS, LANES), F32)
    for b in range(NBANDS):
        low, high = edges[b], edges[b + 1]
        inside = jnp.logical_and(band == b, jnp.logical_and(bins >= low, bins < high))
        select = jnp.where(inside, 1.0, select)
        count = jnp.full((NBANDS, LANES), high - low, jnp.int32).astype(F32)
        width_of = jnp.where(iota((NBANDS, LANES), 0) == b, count, width_of)
    for i in range(2):
        sel[i * LANES : (i + 1) * LANES] = select.astype(BF16)
    widths[...] = width_of
    place = iota((ROWS, LANES), 0)
    for i, lengths in enumerate((sta, lta)):
        length = jnp.zeros((ROWS, LANES), jnp.int32)
        for c in range(ROWS):
            length = jnp.where(place == c, lengths[me * ROWS + c], length)
        turn[i] = length
        scale[i] = 1.0 / length.astype(F32)

    def receive(chunk):
        @pl.loop(0, STEP)
        def _(n):
            s = chunk * STEP + n

            @pl.when(s != me)
            def _():
                pltpu.make_async_remote_copy(
                    src_ref=ga.at[s], dst_ref=r.at[s + 1], send_sem=send_sem.at[s],
                    recv_sem=recv_sem.at[s], device_id=(s, g), device_id_type=MESH).wait_recv()

    rows = STEP * ROWS

    def compute(chunk):
        s0 = chunk * STEP

        def part(slab, q):
            return r[pl.ds(s0 + slab, STEP), :, q * LANES : (q + 1) * LANES].reshape(rows, LANES)

        mine = [part(1, q) for q in range(4)]
        ahead = r[pl.ds(s0, 1), :, LANES:].reshape(ROWS, 3 * LANES)
        windows = stack(
            lanes(ahead, mine[0][:ROWS]),
            lanes(part(0, 3), *mine[:3]),
            lanes(*mine[1:], part(2, 0)),
        )
        filtered = dot(windows, toep[...])
        high, low = split(filtered[ROWS:], 2)
        spectrum = dot(lanes(high, low, high), table[...])
        power = spectrum[:, :LANES] * spectrum[:, :LANES] + spectrum[:, LANES:] * spectrum[:, LANES:]
        total = dot(lanes(*split(power, 2)), sel[...])
        for n in range(STEP):
            for f in range(2):
                at = pl.multiple_of(((s0 + n) * 2 + f) * ROWS, ROWS)
                begin = f * rows + n * ROWS
                bands[pl.ds(at, ROWS), :] = total[begin : begin + ROWS]
        energy = filtered * filtered
        started = jnp.where(s0 > 0, 1.0, 0.0)
        energy = stack(energy[:ROWS] * started, energy[ROWS:])
        running = dot(lanes(*split(energy, 3)), sums[...])
        back = running[:ROWS, 3 * LANES :]
        first, second = running[ROWS : ROWS + rows], running[ROWS + rows :]
        ups = [first[:, :LANES], first[:, LANES:FRAME], second[:, :LANES], second[:, LANES:FRAME]]
        downs = [first[:, FRAME : 3 * LANES], first[:, 3 * LANES :], second[:, FRAME : 3 * LANES], second[:, 3 * LANES :]]
        downs = [stack(back, downs[3][: rows - ROWS])] + downs[:3]
        lane = iota((rows, LANES), 1)
        means = []
        for i in range(2):
            length = stack(*[turn[i]] * STEP)
            inverse = stack(*[scale[i]] * STEP)
            kept = lane < LANES - length
            source = (lane + (LANES - length)) % LANES
            means.append([
                (up - jnp.take_along_axis(jnp.where(kept, up, down), source, axis=1)) * inverse
                for up, down in zip(ups, downs)
            ])
        for q in range(4):
            ratio = (means[0][q] / jnp.maximum(means[1][q], 0.5)).astype(BF16)
            for n in range(STEP):
                at = pl.multiple_of((s0 + n) * 4 * LANES + q * LANES, LANES)
                ratio_out[:, pl.ds(at, LANES)] = ratio[n * ROWS : (n + 1) * ROWS]

    chunks = slabs // STEP
    begin = (own * 4 + STEP - 4) // STEP
    receive(begin % chunks)
    receive((begin + 1) % chunks)

    @pl.loop(1, chunks - 1)
    def _(i):
        receive((begin + i + 1) % chunks)
        compute((begin + i) % chunks)

    @pl.loop(chunks - 1, chunks + 1)
    def _(i):
        compute((begin + i) % chunks)

    frames = 2 * slabs

    @pl.loop(0, ROWS)
    def _(c):
        mean = bands[pl.ds(c, frames, stride=ROWS), :].T[:NBANDS] / widths[:, :frames]
        sig_out[c] = jnp.log1p(mean / FRAME)

    @pl.when(has_hi)
    def _():
        to_hi().wait_send()

    @pl.when(has_lo)
    def _():
        to_lo().wait_send()

    @pl.loop(1, slabs)
    def _(k):
        send((me + k) % slabs).wait_send()


def body(traces, fir_taps, gauge_half, sta_length, lta_length, band_edges):
    slabs, groups = lax.axis_size("tm"), lax.axis_size("grp")
    chans, local = traces.shape
    taps = jnp.pad(fir_taps.astype(F32), (REACH, 2 * FRAME - REACH - NTAPS))[None, :]
    half = gauge_half.reshape(-1, LANES)
    table = jnp.asarray(spectral_table())
    total = slabs * local
    vmem = pl.BlockSpec(memory_space=pltpu.VMEM)
    hbm = pl.BlockSpec(memory_space=pltpu.HBM)
    dma = pltpu.SemaphoreType.DMA
    ratio, signature = pl.pallas_call(
        functools.partial(kernel, slabs, groups),
        out_shape=(
            jax.ShapeDtypeStruct((ROWS, total), BF16),
            jax.ShapeDtypeStruct((ROWS, NBANDS, total // FRAME), F32),
        ),
        in_specs=[hbm] * 7,
        out_specs=(vmem, vmem),
        scratch_shapes=[
            pltpu.VMEM((chans, local), BF16),
            pltpu.VMEM((slabs, ROWS, local), BF16),
            pltpu.VMEM((slabs + 2, ROWS, local), BF16),
            pltpu.VMEM((ROWS, local), BF16),
            pltpu.VMEM((ROWS, local), BF16),
            pltpu.VMEM(taps.shape, taps.dtype),
            pltpu.VMEM(half.shape, half.dtype),
            pltpu.VMEM(table.shape, BF16),
            pltpu.VMEM((2 * FRAME, FRAME), BF16),
            pltpu.VMEM((3 * FRAME, 2 * FRAME), BF16),
            pltpu.VMEM((2 * LANES, LANES), BF16),
            pltpu.VMEM((NBANDS, LANES), F32),
            pltpu.VMEM((2, ROWS, LANES), jnp.int32),
            pltpu.VMEM((2, ROWS, LANES), F32),
            pltpu.VMEM((2 * slabs * ROWS, LANES), F32),
            pltpu.SMEM(sta_length.shape, jnp.int32),
            pltpu.SMEM(lta_length.shape, jnp.int32),
            pltpu.SMEM(band_edges.shape, jnp.int32),
            dma((7,)),
            dma((slabs,)),
            dma((slabs,)),
            dma((2,)),
            dma((2,)),
        ],
        compiler_params=pltpu.CompilerParams(
            collective_id=0, has_side_effects=True, vmem_limit_bytes=62 * 2**20
        ),
        cost_estimate=pl.CostEstimate(flops=4 * 10**9, bytes_accessed=3 * 2**20, transcendentals=0),
    )(traces, taps, half, sta_length, lta_length, band_edges, table)
    return ratio[None], signature[None]


def solution(mesh):
    in_specs = (P("grp", "tm"), P(), P("grp"), P("grp"), P("grp"), P())
    out_specs = (P("grp", "tm", None), P("grp", "tm", None, None))
    return jax.shard_map(body, mesh=mesh, in_specs=in_specs, out_specs=out_specs, check_vma=False)
```

time: 59 us -> 51.8 us (0.88)
  Pallas kernels: 52 us -> 46.8 us
  local copies, waits for them, and re-layouts: 4.64 us -> 3.58 us
  other arithmetic: 1.46 us -> 0.65 us
    pallas_call x1, Pallas kernels: 52 us -> 46.8 us  [body(): pl.pallas_call(functools.partial(kernel, slabs, groups), out_shape=(jax.S...]
    unnamed x14 -> x6, local copies, waits for them, and re-layouts: 4.64 us -> 3.58 us
    reshape x1 -> x0, other arithmetic: 0.73 us -> none  [body(): half = jnp.pad(half, (0, -chans % LANES)).reshape(-1, LANES)]
where the time goes in v2:
time: 51.8 us; the launch traced here: 51.7 us
  Pallas kernels  46.8 us (90%)
  local copies, waits for them, and re-layouts  3.58 us (7%)
  between operations  0.66 us (1%)
  other arithmetic  0.65 us (1%)
    pallas_call x1, Pallas kernels, body(): pl.pallas_call(functools.partial(kernel, slabs, groups), out_shape=(jax.S...  46.8 us
    unnamed x6, local copies, waits for them, and re-layouts  3.58 us

profile of v2, /device:TPU:33, one launch (start us, length us, event | category | flops | bytes accessed | tf_op | source)
XLA Modules:
  0.0 51.7 jit_solution(12551222651101423697)
XLA Ops:
  0.6 0.0 copy-start.1
  0.6 0.6 %copy-done.1 = bf16[129]{0:T(256)(128)(2,1)S(1)} copy-done((bf16[129]{0:T(256)(128)(2,1)S(1)}, bf16[129]{0:T(256)(128)(2,1)}, u32[]{:S(2)}) %copy-start.1) | copy-done | bytes 282
  1.3 0.7 %pad_convert_fusion = f32[512]{0:T(512)} fusion(bf16[129]{0:T(256)(128)(2,1)S(1)} %copy-done.1), kind=kLoop, calls=%fused_computation | loop fusion | flops 512 | bytes 2306 | tf_op jit(solution)/shard_map/broadcast_in_dim | solution.py:326
  1.9 46.8 %shard_map.86 = (bf16[16,32768]{1,0:T(8,128)(2,1)}, f32[16,8,128]{2,1,0:T(8,128)}) custom-call(bf16[1024,512]{1,0:T(8,128)(2,1)} %traces.1, f32[1,512]{1,0:T(1,128)} %bitcast.6, s32[8,128]{1,0:T(8,128)} %bitcast.7, s32[1024]{0:T(1024)} %sta_in.1, s32[1024]{0:T(1024)} %lta_in.1, s32[9]{0:T(128)} %edges_in.1, bf16[768,256]{1,0:T(8,128)(2,1)} %constant.6.clone.table_in), custom_call_target="tpu_custom_call" | custom-call | flops 4000000000 | bytes 3145728 | tf_op jit(solution)/shard_map/pallas_call | solution.py:333
  48.8 0.0 copy-start
  48.8 2.3 %copy.11 = bf16[1,16,32768]{2,1,0:T(8,128)(2,1)} copy(bf16[1,16,32768]{2,1,0:T(8,128)(2,1)} %bitcast.4) | data formatting | bytes 2097152
  51.1 0.0 copy-done
  51.1 0.6 %copy.12 = f32[1,16,8,128]{3,2,1,0:T(8,128)} copy(f32[1,16,8,128]{3,2,1,0:T(8,128)S(1)} %bitcast.5) | data formatting | bytes 131072
Async XLA Ops:
  0.6 0.7 %copy-start.1 = (bf16[129]{0:T(256)(128)(2,1)S(1)}, bf16[129]{0:T(256)(128)(2,1)}, u32[]{:S(2)}) copy-start(bf16[129]{0:T(256)(128)(2,1)} %param.8) | copy-start | bytes 778
  48.8 2.3 %copy-start = (f32[16,8,128]{2,1,0:T(8,128)S(1)}, f32[16,8,128]{2,1,0:T(8,128)}, u32[]{:S(2)}) copy-start(f32[16,8,128]{2,1,0:T(8,128)} %get-tuple-element.5) | copy-start | bytes 196612

commit v3 on v2

--- a/solution.py
+++ b/solution.py
@@ -65,11 +65,27 @@
     return jnp.where(rel == 0.0, 1.0, side).astype(BF16)
 
 
+def wrap(i, n):
+    return jnp.where(i >= n, i - n, i)
+
+
+def finish(ratio, bands, widths, ratio_out, sig_out, sig, sems):
+    whole = pltpu.make_async_copy(ratio, ratio_out.at[0], sems.at[0])
+    whole.start()
+    for c in range(ROWS):
+        mean = bands[pl.ds(c, sig.shape[2], stride=ROWS), :].T[:NBANDS] / widths[:, : sig.shape[2]]
+        sig[c] = jnp.log1p(mean / FRAME)
+    logs = pltpu.make_async_copy(sig, sig_out.at[0], sems.at[1])
+    logs.start()
+    whole.wait()
+    logs.wait()
+
+
 def kernel(
     slabs, groups,
     traces, taps_in, half_in, sta_in, lta_in, edges_in, table_in,
-    ratio_out, sig_out,
-    x, ga, r, lo_halo, hi_halo, taps, half, table, toep, sums, sel, widths, turn, scale, bands,
+    ratio_out, bands, widths,
+    x, ga, r, lo_halo, hi_halo, taps, half, table, toep, sums, sel, turn, shorter, scale,
     sta, lta, edges,
     in_sem, send_sem, recv_sem, hsend, hrecv,
 ):
@@ -91,7 +107,7 @@
 
     @pl.loop(1, slabs)
     def _(k):
-        pl.semaphore_signal(barrier, inc=1, device_id=((me + k) % slabs, g), device_id_type=MESH)
+        pl.semaphore_signal(barrier, inc=1, device_id=(wrap(me + k, slabs), g), device_id_type=MESH)
 
     @pl.when(has_lo)
     def _():
@@ -142,19 +158,26 @@
             src_ref=ga.at[d], dst_ref=r.at[me + 1], send_sem=send_sem.at[d],
             recv_sem=recv_sem.at[me], device_id=(d, g), device_id_type=MESH)
 
-    def target(k, e):
-        flip = (me // 2 % 2 + 1 + e // 2) % 2
-        return (own + columns - k) % columns * 4 + flip * 2 + e % 2
+    across = (own * 2 + 1 - me // 2 % 2) * 2
+    beside = (own * 2 + me // 2 % 2) * 2
+
+    def send_column(k, allowed):
+        shift = jnp.where(k > own, columns - k, -k) * 4
+        for e in range(4):
+            d = (across if e < 2 else beside) + shift + e % 2
+
+            @pl.when(allowed(d))
+            def _():
+                send(d).start()
+
+    def on_edge(d):
+        return jnp.logical_or(d == 0, d == slabs - 1)
 
     early = columns // 2
 
-    @pl.loop(0, early * 4)
-    def _(i):
-        d = target(i // 4, i % 4)
-
-        @pl.when(jnp.logical_and(d != me, jnp.logical_and(d != 0, d != slabs - 1)))
-        def _():
-            send(d).start()
+    @pl.loop(0, early)
+    def _(k):
+        send_column(k, lambda d: jnp.logical_and(d != me, jnp.logical_not(on_edge(d))))
 
     @pl.when(has_lo)
     def _():
@@ -178,31 +201,32 @@
     m = gauge_matrix(half_column(chans // block - 1)[block - ROWS :], LANES, edge - ROWS)
     ga[slabs - 1] = dot(m, stack(x[chans - edge :, :], hi_halo[...])).astype(BF16)
 
-    @pl.loop(0, columns * 4)
-    def _(i):
-        d = target(i // 4, i % 4)
-        edge_row = jnp.logical_or(d == 0, d == slabs - 1)
-
-        @pl.when(jnp.logical_and(d != me, jnp.logical_or(i >= early * 4, edge_row)))
+    for d in (0, slabs - 1):
+        back = wrap(own + columns - d // 4, columns)
+
+        @pl.when(jnp.logical_and(d != me, back < early))
         def _():
             send(d).start()
+
+    @pl.loop(early, columns)
+    def _(k):
+        send_column(k, lambda d: d != me)
 
     r[pl.ds(me + 1, 1)] = ga[pl.ds(me, 1)]
     r[0] = jnp.zeros(r.shape[1:], BF16)
     r[slabs + 1] = jnp.zeros(r.shape[1:], BF16)
     for load in loads[2:]:
         load.wait()
-    row = jnp.broadcast_to(taps[...], (FRAME, 2 * FRAME))
-    toep[...] = pltpu.roll(row, 0, 1, stride=1, stride_axis=0).T.astype(BF16)
-    earlier = iota((FRAME, 2 * FRAME), 0)
-    sample = iota((FRAME, 2 * FRAME), 1)
-    tile = sample // LANES % 2 == earlier // LANES
-    through = earlier % LANES <= sample % LANES
-    upto = jnp.where(jnp.logical_and(tile, through), 1.0, 0.0)
-    after = jnp.where(jnp.logical_and(tile, jnp.logical_not(through)), -1.0, 0.0)
-    both = jnp.where(sample < FRAME, upto, after).astype(BF16)
+    tap = taps[...].astype(F32).reshape(1, NTAPS)
+    row = jnp.concatenate([tap, jnp.zeros((1, 2 * FRAME - NTAPS), F32)], axis=1)
+    row = jnp.broadcast_to(row, (FRAME, 2 * FRAME))
+    toep[...] = pltpu.roll(row, REACH, 1, stride=1, stride_axis=0).T.astype(BF16)
+    earlier = iota((FRAME, FRAME), 0)
+    sample = iota((FRAME, FRAME), 1)
+    tile = sample // LANES == earlier // LANES
+    upto = jnp.where(jnp.logical_and(tile, earlier <= sample), 1.0, 0.0).astype(BF16)
     for i in range(3):
-        sums[i * FRAME : (i + 1) * FRAME] = both
+        sums[i * FRAME : (i + 1) * FRAME] = upto
     bins = iota((LANES, LANES), 0)
     band = iota((LANES, LANES), 1)
     select = jnp.zeros((LANES, LANES), F32)
@@ -221,7 +245,9 @@
         length = jnp.zeros((ROWS, LANES), jnp.int32)
         for c in range(ROWS):
             length = jnp.where(place == c, lengths[me * ROWS + c], length)
-        turn[i] = length
+        source = iota((ROWS, LANES), 1) - length
+        turn[i] = jnp.where(source < 0, source + LANES, source)
+        shorter[i] = LANES - length
         scale[i] = 1.0 / length.astype(F32)
 
     def receive(chunk):
@@ -264,18 +290,17 @@
         started = jnp.where(s0 > 0, 1.0, 0.0)
         energy = stack(energy[:ROWS] * started, energy[ROWS:])
         running = dot(lanes(*split(energy, 3)), sums[...])
-        back = running[:ROWS, 3 * LANES :]
+        back = running[:ROWS, LANES:]
         first, second = running[ROWS : ROWS + rows], running[ROWS + rows :]
-        ups = [first[:, :LANES], first[:, LANES:FRAME], second[:, :LANES], second[:, LANES:FRAME]]
-        downs = [first[:, FRAME : 3 * LANES], first[:, 3 * LANES :], second[:, FRAME : 3 * LANES], second[:, 3 * LANES :]]
-        downs = [stack(back, downs[3][: rows - ROWS])] + downs[:3]
+        ups = [first[:, :LANES], first[:, LANES:], second[:, :LANES], second[:, LANES:]]
+        downs = [stack(back, ups[3][: rows - ROWS])] + ups[:3]
+        downs = [down - down[:, LANES - 1 :] for down in downs]
         lane = iota((rows, LANES), 1)
         means = []
         for i in range(2):
-            length = stack(*[turn[i]] * STEP)
+            kept = lane < stack(*[shorter[i]] * STEP)
             inverse = stack(*[scale[i]] * STEP)
-            kept = lane < LANES - length
-            source = (lane + (LANES - length)) % LANES
+            source = stack(*[turn[i]] * STEP)
             means.append([
                 (up - jnp.take_along_axis(jnp.where(kept, up, down), source, axis=1)) * inverse
                 for up, down in zip(ups, downs)
@@ -300,13 +325,6 @@
     def _(i):
         compute((begin + i) % chunks)
 
-    frames = 2 * slabs
-
-    @pl.loop(0, ROWS)
-    def _(c):
-        mean = bands[pl.ds(c, frames, stride=ROWS), :].T[:NBANDS] / widths[:, :frames]
-        sig_out[c] = jnp.log1p(mean / FRAME)
-
     @pl.when(has_hi)
     def _():
         to_hi().wait_send()
@@ -317,27 +335,30 @@
 
     @pl.loop(1, slabs)
     def _(k):
-        send((me + k) % slabs).wait_send()
+        send(wrap(me + k, slabs)).wait_send()
 
 
 def body(traces, fir_taps, gauge_half, sta_length, lta_length, band_edges):
     slabs, groups = lax.axis_size("tm"), lax.axis_size("grp")
     chans, local = traces.shape
-    taps = jnp.pad(fir_taps.astype(F32), (REACH, 2 * FRAME - REACH - NTAPS))[None, :]
+    taps = fir_taps
     half = gauge_half.reshape(-1, LANES)
     table = jnp.asarray(spectral_table())
     total = slabs * local
     vmem = pl.BlockSpec(memory_space=pltpu.VMEM)
     hbm = pl.BlockSpec(memory_space=pltpu.HBM)
     dma = pltpu.SemaphoreType.DMA
-    ratio, signature = pl.pallas_call(
+    operands = (traces, taps, half, sta_length, lta_length, band_edges, table)
+    operands = [pltpu.with_memory_space_constraint(a, pltpu.HBM) for a in operands]
+    ratio, bands, widths = pl.pallas_call(
         functools.partial(kernel, slabs, groups),
         out_shape=(
             jax.ShapeDtypeStruct((ROWS, total), BF16),
-            jax.ShapeDtypeStruct((ROWS, NBANDS, total // FRAME), F32),
+            jax.ShapeDtypeStruct((total // FRAME * ROWS, LANES), F32),
+            jax.ShapeDtypeStruct((NBANDS, LANES), F32),
         ),
         in_specs=[hbm] * 7,
-        out_specs=(vmem, vmem),
+        out_specs=(vmem, vmem, vmem),
         scratch_shapes=[
             pltpu.VMEM((chans, local), BF16),
             pltpu.VMEM((slabs, ROWS, local), BF16),
@@ -348,12 +369,11 @@
             pltpu.VMEM(half.shape, half.dtype),
             pltpu.VMEM(table.shape, BF16),
             pltpu.VMEM((2 * FRAME, FRAME), BF16),
-            pltpu.VMEM((3 * FRAME, 2 * FRAME), BF16),
+            pltpu.VMEM((3 * FRAME, FRAME), BF16),
             pltpu.VMEM((2 * LANES, LANES), BF16),
-            pltpu.VMEM((NBANDS, LANES), F32),
+            pltpu.VMEM((2, ROWS, LANES), jnp.int32),
             pltpu.VMEM((2, ROWS, LANES), jnp.int32),
             pltpu.VMEM((2, ROWS, LANES), F32),
-            pltpu.VMEM((2 * slabs * ROWS, LANES), F32),
             pltpu.SMEM(sta_length.shape, jnp.int32),
             pltpu.SMEM(lta_length.shape, jnp.int32),
             pltpu.SMEM(band_edges.shape, jnp.int32),
@@ -364,11 +384,22 @@
             dma((2,)),
         ],
         compiler_params=pltpu.CompilerParams(
-            collective_id=0, has_side_effects=True, vmem_limit_bytes=62 * 2**20
+            collective_id=0, has_side_effects=True, vmem_limit_bytes=40 * 2**20
         ),
         cost_estimate=pl.CostEstimate(flops=4 * 10**9, bytes_accessed=3 * 2**20, transcendentals=0),
-    )(traces, taps, half, sta_length, lta_length, band_edges, table)
-    return ratio[None], signature[None]
+    )(*operands)
+    frames = total // FRAME
+    return pl.pallas_call(
+        finish,
+        out_shape=(
+            jax.ShapeDtypeStruct((1, ROWS, total), BF16),
+            jax.ShapeDtypeStruct((1, ROWS, NBANDS, frames), F32),
+        ),
+        in_specs=[vmem] * 3,
+        out_specs=(hbm, hbm),
+        scratch_shapes=[pltpu.VMEM((ROWS, NBANDS, frames), F32), dma((2,))],
+        compiler_params=pltpu.CompilerParams(vmem_limit_bytes=8 * 2**20),
+    )(ratio, bands, widths)
 
 
 def solution(mesh):

time: 51.8 us -> 46.2 us (0.89)
  local copies, waits for them, and re-layouts: 3.58 us -> 0 us
  Pallas kernels: 46.8 us -> 45.4 us
  other arithmetic: 0.65 us -> 0 us
    unnamed x6 -> x0, local copies, waits for them, and re-layouts: 3.58 us -> none
    pallas_call x1, Pallas kernels: 46.8 us -> 44.4 us  [body(): pl.pallas_call(functools.partial(kernel, slabs, groups), out_shape=(jax.S...]
    pallas_call x0 -> x1, Pallas kernels: none -> 1.03 us  [body(): pl.pallas_call(finish, out_shape=(jax.ShapeDtypeStruct((1, ROWS, total),...]
    broadcast_in_dim x1 -> x0, other arithmetic: 0.65 us -> none  [body(): jnp.pad(fir_taps.astype(F32), (REACH, 2 * FRAME - REACH - NTAPS))[None, :]]
where the time goes in v3:
time: 46.2 us; the launch traced here: 46.1 us
  Pallas kernels  45.4 us (98%)
  between operations  0.64 us (1%)
    pallas_call x1, Pallas kernels, body(): pl.pallas_call(functools.partial(kernel, slabs, groups), out_shape=(jax.S...  44.4 us
    pallas_call x1, Pallas kernels, body(): pl.pallas_call(finish, out_shape=(jax.ShapeDtypeStruct((1, ROWS, total),...  1.03 us

profile of v3, /device:TPU:33, one launch (start us, length us, event | category | flops | bytes accessed | tf_op | source)
XLA Modules:
  0.0 46.1 jit_solution(9234478183183831476)
XLA Ops:
  0.6 44.4 %shard_map.86 = (bf16[16,32768]{1,0:T(8,128)(2,1)S(1)}, f32[2048,128]{1,0:T(8,128)S(1)}, f32[8,128]{1,0:T(8,128)S(1)}) custom-call(bf16[1024,512]{1,0:T(8,128)(2,1)} %traces.1, bf16[129]{0:T(256)(128)(2,1)} %taps_in.1, s32[8,128]{1,0:T(8,128)} %bitcast.1, s32[1024]{0:T(1024)} %sta_in.1, s32[1024]{0:T(1024)} %lta_in.1, s32[9]{0:T(128)} %edges_in.1, ...), custom_call_target="tpu_custom_call" | custom-call | flops 4000000000 | bytes 3145728 | tf_op jit(solution)/shard_map/pallas_call | solution.py:353
  45.0 1.0 %shard_map.87 = (bf16[1,16,32768]{2,1,0:T(8,128)(2,1)}, f32[1,16,8,128]{3,2,1,0:T(8,128)}) custom-call(bf16[16,32768]{1,0:T(8,128)(2,1)S(1)} %get-tuple-element.5.ratio, f32[2048,128]{1,0:T(8,128)S(1)} %get-tuple-element.6.bands, f32[8,128]{1,0:T(8,128)S(1)} %get-tuple-element.7.widths), custom_call_target="tpu_custom_call" | custom-call | tf_op jit(solution)/shard_map/pallas_call | solution.py:392

commit v4 on v3

--- a/solution.py
+++ b/solution.py
@@ -99,24 +99,24 @@
     has_lo = g > 0
     has_hi = g < groups - 1
 
+    barrier = pltpu.get_barrier_semaphore()
+
+    @pl.loop(1, slabs, unroll=True)
+    def _(k):
+        pl.semaphore_signal(barrier, inc=1, device_id=(wrap(me + k, slabs), g), device_id_type=MESH)
+
+    @pl.when(has_lo)
+    def _():
+        pl.semaphore_signal(barrier, inc=1, device_id=(me, g - 1), device_id_type=MESH)
+
+    @pl.when(has_hi)
+    def _():
+        pl.semaphore_signal(barrier, inc=1, device_id=(me, g + 1), device_id_type=MESH)
+
     pairs = [(traces, x), (half_in, half), (table_in, table), (taps_in, taps), (sta_in, sta), (lta_in, lta), (edges_in, edges)]
     loads = [pltpu.make_async_copy(a, b, in_sem.at[i]) for i, (a, b) in enumerate(pairs)]
     for load in loads:
         load.start()
-    barrier = pltpu.get_barrier_semaphore()
-
-    @pl.loop(1, slabs)
-    def _(k):
-        pl.semaphore_signal(barrier, inc=1, device_id=(wrap(me + k, slabs), g), device_id_type=MESH)
-
-    @pl.when(has_lo)
-    def _():
-        pl.semaphore_signal(barrier, inc=1, device_id=(me, g - 1), device_id_type=MESH)
-
-    @pl.when(has_hi)
-    def _():
-        pl.semaphore_signal(barrier, inc=1, device_id=(me, g + 1), device_id_type=MESH)
-
     def half_column(i):
         row = jnp.broadcast_to(half[pl.ds(i, 1), :].astype(F32), (LANES, LANES))
         return row.T
@@ -153,10 +153,12 @@
     def _():
         to_lo().start()
 
-    def send(d):
+    seat = me % 4
+
+    def send(d, back):
         return pltpu.make_async_remote_copy(
-            src_ref=ga.at[d], dst_ref=r.at[me + 1], send_sem=send_sem.at[d],
-            recv_sem=recv_sem.at[me], device_id=(d, g), device_id_type=MESH)
+            src_ref=ga.at[d], dst_ref=r.at[back * 4 + seat], send_sem=send_sem,
+            recv_sem=recv_sem.at[back], device_id=(d, g), device_id_type=MESH)
 
     across = (own * 2 + 1 - me // 2 % 2) * 2
     beside = (own * 2 + me // 2 % 2) * 2
@@ -168,7 +170,7 @@
 
             @pl.when(allowed(d))
             def _():
-                send(d).start()
+                send(d, k).start()
 
     def on_edge(d):
         return jnp.logical_or(d == 0, d == slabs - 1)
@@ -206,15 +208,13 @@
 
         @pl.when(jnp.logical_and(d != me, back < early))
         def _():
-            send(d).start()
+            send(d, back).start()
 
     @pl.loop(early, columns)
     def _(k):
         send_column(k, lambda d: d != me)
 
-    r[pl.ds(me + 1, 1)] = ga[pl.ds(me, 1)]
-    r[0] = jnp.zeros(r.shape[1:], BF16)
-    r[slabs + 1] = jnp.zeros(r.shape[1:], BF16)
+    r[pl.ds(seat, 1)] = ga[pl.ds(me, 1)]
     for load in loads[2:]:
         load.wait()
     tap = taps[...].astype(F32).reshape(1, NTAPS)
@@ -250,31 +250,30 @@
         shorter[i] = LANES - length
         scale[i] = 1.0 / length.astype(F32)
 
-    def receive(chunk):
-        @pl.loop(0, STEP)
-        def _(n):
-            s = chunk * STEP + n
-
-            @pl.when(s != me)
-            def _():
-                pltpu.make_async_remote_copy(
-                    src_ref=ga.at[s], dst_ref=r.at[s + 1], send_sem=send_sem.at[s],
-                    recv_sem=recv_sem.at[s], device_id=(s, g), device_id_type=MESH).wait_recv()
+    def receive(column, count):
+        pltpu.make_async_remote_copy(
+            src_ref=ga.at[pl.ds(0, count)], dst_ref=r.at[pl.ds(column * 4, count)], send_sem=send_sem,
+            recv_sem=recv_sem.at[column], device_id=(wrap(me + 1, slabs), g), device_id_type=MESH).wait_recv()
 
     rows = STEP * ROWS
 
-    def compute(chunk):
-        s0 = chunk * STEP
-
-        def part(slab, q):
-            return r[pl.ds(s0 + slab, STEP), :, q * LANES : (q + 1) * LANES].reshape(rows, LANES)
-
+    def compute(i):
+        base = i * STEP
+        first = (own * 4 + base + 1) % slabs
+        place = [wrap(first + n, slabs) for n in range(STEP)]
+
+        def part(o, q):
+            return r[pl.ds(base + o, STEP), :, q * LANES : (q + 1) * LANES].reshape(rows, LANES)
+
+        slab = iota((rows, LANES), 0) // ROWS
+        follows = jnp.where(slab == wrap(slabs - first, slabs), 0.0, 1.0)
+        goes_on = jnp.where(slab == slabs - 1 - first, 0.0, 1.0)
         mine = [part(1, q) for q in range(4)]
-        ahead = r[pl.ds(s0, 1), :, LANES:].reshape(ROWS, 3 * LANES)
+        ahead = r[pl.ds(base, 1), :, LANES:].reshape(ROWS, 3 * LANES)
         windows = stack(
             lanes(ahead, mine[0][:ROWS]),
-            lanes(part(0, 3), *mine[:3]),
-            lanes(*mine[1:], part(2, 0)),
+            lanes(part(0, 3) * follows.astype(BF16), *mine[:3]),
+            lanes(*mine[1:], part(2, 0) * goes_on.astype(BF16)),
         )
         filtered = dot(windows, toep[...])
         high, low = split(filtered[ROWS:], 2)
@@ -283,17 +282,15 @@
         total = dot(lanes(*split(power, 2)), sel[...])
         for n in range(STEP):
             for f in range(2):
-                at = pl.multiple_of(((s0 + n) * 2 + f) * ROWS, ROWS)
+                at = pl.multiple_of((place[n] * 2 + f) * ROWS, ROWS)
                 begin = f * rows + n * ROWS
                 bands[pl.ds(at, ROWS), :] = total[begin : begin + ROWS]
         energy = filtered * filtered
-        started = jnp.where(s0 > 0, 1.0, 0.0)
-        energy = stack(energy[:ROWS] * started, energy[ROWS:])
         running = dot(lanes(*split(energy, 3)), sums[...])
         back = running[:ROWS, LANES:]
-        first, second = running[ROWS : ROWS + rows], running[ROWS + rows :]
-        ups = [first[:, :LANES], first[:, LANES:], second[:, :LANES], second[:, LANES:]]
-        downs = [stack(back, ups[3][: rows - ROWS])] + ups[:3]
+        left, right = running[ROWS : ROWS + rows], running[ROWS + rows :]
+        ups = [left[:, :LANES], left[:, LANES:], right[:, :LANES], right[:, LANES:]]
+        downs = [stack(back, ups[3][: rows - ROWS]) * follows] + ups[:3]
         downs = [down - down[:, LANES - 1 :] for down in downs]
         lane = iota((rows, LANES), 1)
         means = []
@@ -308,22 +305,23 @@
         for q in range(4):
             ratio = (means[0][q] / jnp.maximum(means[1][q], 0.5)).astype(BF16)
             for n in range(STEP):
-                at = pl.multiple_of((s0 + n) * 4 * LANES + q * LANES, LANES)
+                at = pl.multiple_of(place[n] * 4 * LANES + q * LANES, LANES)
                 ratio_out[:, pl.ds(at, LANES)] = ratio[n * ROWS : (n + 1) * ROWS]
 
-    chunks = slabs // STEP
-    begin = (own * 4 + STEP - 4) // STEP
-    receive(begin % chunks)
-    receive((begin + 1) % chunks)
-
-    @pl.loop(1, chunks - 1)
+    receive(0, 3)
+    r[slabs] = r[0]
+    r[slabs + 1] = r[1]
+
+    @pl.loop(0, slabs // STEP)
     def _(i):
-        receive((begin + i + 1) % chunks)
-        compute((begin + i) % chunks)
-
-    @pl.loop(chunks - 1, chunks + 1)
-    def _(i):
-        compute((begin + i) % chunks)
+        for n in range(STEP // 4):
+            column = i * (STEP // 4) + 1 + n
+
+            @pl.when(column < columns)
+            def _():
+                receive(column, 4)
+
+        compute(i)
 
     @pl.when(has_hi)
     def _():
@@ -333,9 +331,9 @@
     def _():
         to_lo().wait_send()
 
-    @pl.loop(1, slabs)
-    def _(k):
-        send(wrap(me + k, slabs)).wait_send()
+    pltpu.make_async_remote_copy(
+        src_ref=ga.at[pl.ds(0, slabs - 1)], dst_ref=r.at[pl.ds(0, slabs - 1)], send_sem=send_sem,
+        recv_sem=recv_sem.at[0], device_id=(wrap(me + 1, slabs), g), device_id_type=MESH).wait_send()
 
 
 def body(traces, fir_taps, gauge_half, sta_length, lta_length, band_edges):
@@ -378,8 +376,8 @@
             pltpu.SMEM(lta_length.shape, jnp.int32),
             pltpu.SMEM(band_edges.shape, jnp.int32),
             dma((7,)),
-            dma((slabs,)),
-            dma((slabs,)),
+            dma,
+            dma((slabs // 4,)),
             dma((2,)),
             dma((2,)),
         ],

time: 46.2 us -> 43.4 us (0.939)
  Pallas kernels: 45.4 us -> 42.7 us
    pallas_call x1, Pallas kernels: 44.4 us -> 41.7 us  [body(): pl.pallas_call(functools.partial(kernel, slabs, groups), out_shape=(jax.S...]
where the time goes in v4:
time: 43.4 us; the launch traced here: 43.3 us
  Pallas kernels  42.7 us (98%)
  between operations  0.64 us (1%)
    pallas_call x1, Pallas kernels, body(): pl.pallas_call(functools.partial(kernel, slabs, groups), out_shape=(jax.S...  41.7 us
    pallas_call x1, Pallas kernels, body(): pl.pallas_call(finish, out_shape=(jax.ShapeDtypeStruct((1, ROWS, total),...  1.03 us

profile of v4, /device:TPU:33, one launch (start us, length us, event | category | flops | bytes accessed | tf_op | source)
XLA Modules:
  0.0 43.3 jit_solution(9605866209606742669)
XLA Ops:
  0.6 41.7 %shard_map.86 = (bf16[16,32768]{1,0:T(8,128)(2,1)S(1)}, f32[2048,128]{1,0:T(8,128)S(1)}, f32[8,128]{1,0:T(8,128)S(1)}) custom-call(bf16[1024,512]{1,0:T(8,128)(2,1)} %traces.1, bf16[129]{0:T(256)(128)(2,1)} %taps_in.1, s32[8,128]{1,0:T(8,128)} %bitcast.1, s32[1024]{0:T(1024)} %sta_in.1, s32[1024]{0:T(1024)} %lta_in.1, s32[9]{0:T(128)} %edges_in.1, ...), custom_call_target="tpu_custom_call" | custom-call | flops 4000000000 | bytes 3145728 | tf_op jit(solution)/shard_map/pallas_call | solution.py:351
  42.3 1.0 %shard_map.87 = (bf16[1,16,32768]{2,1,0:T(8,128)(2,1)}, f32[1,16,8,128]{3,2,1,0:T(8,128)}) custom-call(bf16[16,32768]{1,0:T(8,128)(2,1)S(1)} %get-tuple-element.5.ratio, f32[2048,128]{1,0:T(8,128)S(1)} %get-tuple-element.6.bands, f32[8,128]{1,0:T(8,128)S(1)} %get-tuple-element.7.widths), custom_call_target="tpu_custom_call" | custom-call | tf_op jit(solution)/shard_map/pallas_call | solution.py:390

commit v5 on v4

--- a/solution.py
+++ b/solution.py
@@ -15,7 +15,7 @@
 FRAME = 256
 NBANDS = 8
 ROWS = 16
-STEP = 8
+STEP = 16
 MESH = pl.DeviceIdType.MESH
 F32 = jnp.float32
 BF16 = jnp.bfloat16
@@ -125,7 +125,7 @@
     loads[1].wait()
     width = min(2 * LANES, chans)
 
-    @pl.loop(0, chans // block)
+    @pl.loop(0, chans // block, unroll=4)
     def _(i):
         start = jnp.clip(i * block - REACH, 0, chans - width)
         rows = x[pl.ds(pl.multiple_of(start, ROWS), width), :]
@@ -223,8 +223,7 @@
     toep[...] = pltpu.roll(row, REACH, 1, stride=1, stride_axis=0).T.astype(BF16)
     earlier = iota((FRAME, FRAME), 0)
     sample = iota((FRAME, FRAME), 1)
-    tile = sample // LANES == earlier // LANES
-    upto = jnp.where(jnp.logical_and(tile, earlier <= sample), 1.0, 0.0).astype(BF16)
+    upto = jnp.where(earlier <= sample, 1.0, 0.0).astype(BF16)
     for i in range(3):
         sums[i * FRAME : (i + 1) * FRAME] = upto
     bins = iota((LANES, LANES), 0)
@@ -276,22 +275,16 @@
             lanes(*mine[1:], part(2, 0) * goes_on.astype(BF16)),
         )
         filtered = dot(windows, toep[...])
+        energy = filtered * filtered
+        running = dot(lanes(*split(energy, 3)), sums[...])
         high, low = split(filtered[ROWS:], 2)
         spectrum = dot(lanes(high, low, high), table[...])
         power = spectrum[:, :LANES] * spectrum[:, :LANES] + spectrum[:, LANES:] * spectrum[:, LANES:]
-        total = dot(lanes(*split(power, 2)), sel[...])
-        for n in range(STEP):
-            for f in range(2):
-                at = pl.multiple_of((place[n] * 2 + f) * ROWS, ROWS)
-                begin = f * rows + n * ROWS
-                bands[pl.ds(at, ROWS), :] = total[begin : begin + ROWS]
-        energy = filtered * filtered
-        running = dot(lanes(*split(energy, 3)), sums[...])
         back = running[:ROWS, LANES:]
         left, right = running[ROWS : ROWS + rows], running[ROWS + rows :]
         ups = [left[:, :LANES], left[:, LANES:], right[:, :LANES], right[:, LANES:]]
-        downs = [stack(back, ups[3][: rows - ROWS]) * follows] + ups[:3]
-        downs = [down - down[:, LANES - 1 :] for down in downs]
+        before = stack(back, ups[3][: rows - ROWS]) * follows
+        downs = [before - before[:, LANES - 1 :], ups[0], ups[1] - ups[1][:, LANES - 1 :], ups[2]]
         lane = iota((rows, LANES), 1)
         means = []
         for i in range(2):
@@ -307,6 +300,12 @@
             for n in range(STEP):
                 at = pl.multiple_of(place[n] * 4 * LANES + q * LANES, LANES)
                 ratio_out[:, pl.ds(at, LANES)] = ratio[n * ROWS : (n + 1) * ROWS]
+        total = dot(lanes(*split(power, 2)), sel[...])
+        for n in range(STEP):
+            for f in range(2):
+                at = pl.multiple_of((place[n] * 2 + f) * ROWS, ROWS)
+                begin = f * rows + n * ROWS
+                bands[pl.ds(at, ROWS), :] = total[begin : begin + ROWS]
 
     receive(0, 3)
     r[slabs] = r[0]

time: 43.4 us -> 41.3 us (0.952)
  Pallas kernels: 42.7 us -> 40.5 us
    pallas_call x1, Pallas kernels: 41.7 us -> 39.5 us  [body(): pl.pallas_call(functools.partial(kernel, slabs, groups), out_shape=(jax.S...]
where the time goes in v5:
time: 41.3 us; the launch traced here: 41.2 us
  Pallas kernels  40.5 us (98%)
  between operations  0.64 us (2%)
    pallas_call x1, Pallas kernels, body(): pl.pallas_call(functools.partial(kernel, slabs, groups), out_shape=(jax.S...  39.5 us
    pallas_call x1, Pallas kernels, body(): pl.pallas_call(finish, out_shape=(jax.ShapeDtypeStruct((1, ROWS, total),...  1.03 us

profile of v5, /device:TPU:33, one launch (start us, length us, event | category | flops | bytes accessed | tf_op | source)
XLA Modules:
  0.0 41.2 jit_solution(9559340571386568644)
XLA Ops:
  0.6 39.5 %shard_map.86 = (bf16[16,32768]{1,0:T(8,128)(2,1)S(1)}, f32[2048,128]{1,0:T(8,128)S(1)}, f32[8,128]{1,0:T(8,128)S(1)}) custom-call(bf16[1024,512]{1,0:T(8,128)(2,1)} %traces.1, bf16[129]{0:T(256)(128)(2,1)} %taps_in.1, s32[8,128]{1,0:T(8,128)} %bitcast.1, s32[1024]{0:T(1024)} %sta_in.1, s32[1024]{0:T(1024)} %lta_in.1, s32[9]{0:T(128)} %edges_in.1, ...), custom_call_target="tpu_custom_call" | custom-call | flops 4000000000 | bytes 3145728 | tf_op jit(solution)/shard_map/pallas_call | solution.py:350
  40.1 1.0 %shard_map.87 = (bf16[1,16,32768]{2,1,0:T(8,128)(2,1)}, f32[1,16,8,128]{3,2,1,0:T(8,128)}) custom-call(bf16[16,32768]{1,0:T(8,128)(2,1)S(1)} %get-tuple-element.5.ratio, f32[2048,128]{1,0:T(8,128)S(1)} %get-tuple-element.6.bands, f32[8,128]{1,0:T(8,128)S(1)} %get-tuple-element.7.widths), custom_call_target="tpu_custom_call" | custom-call | tf_op jit(solution)/shard_map/pallas_call | solution.py:389

commit v6 on v5

--- a/solution.py
+++ b/solution.py
@@ -70,14 +70,20 @@
 
 
 def finish(ratio, bands, widths, ratio_out, sig_out, sig, sems):
-    whole = pltpu.make_async_copy(ratio, ratio_out.at[0], sems.at[0])
-    whole.start()
-    for c in range(ROWS):
-        mean = bands[pl.ds(c, sig.shape[2], stride=ROWS), :].T[:NBANDS] / widths[:, : sig.shape[2]]
-        sig[c] = jnp.log1p(mean / FRAME)
-    logs = pltpu.make_async_copy(sig, sig_out.at[0], sems.at[1])
+    size = ratio.shape[1] // 4
+    parts = [
+        pltpu.make_async_copy(
+            ratio.at[:, pl.ds(i * size, size)], ratio_out.at[0, :, pl.ds(i * size, size)], sems.at[i + 1])
+        for i in range(4)
+    ]
+    for part in parts:
+        part.start()
+    mean = bands[...].T.reshape(sig.shape) / widths[:, : sig.shape[2]]
+    sig[...] = jnp.log1p(mean / FRAME)
+    logs = pltpu.make_async_copy(sig, sig_out.at[0], sems.at[0])
     logs.start()
-    whole.wait()
+    for part in parts:
+        part.wait()
     logs.wait()
 
 
@@ -101,7 +107,7 @@
 
     barrier = pltpu.get_barrier_semaphore()
 
-    @pl.loop(1, slabs, unroll=True)
+    @pl.loop(1, slabs, unroll=9)
     def _(k):
         pl.semaphore_signal(barrier, inc=1, device_id=(wrap(me + k, slabs), g), device_id_type=MESH)
 
@@ -232,7 +238,7 @@
     width_of = jnp.ones((NBANDS, LANES), F32)
     for b in range(NBANDS):
         low, high = edges[b], edges[b + 1]
-        inside = jnp.logical_and(band == b, jnp.logical_and(bins >= low, bins < high))
+        inside = jnp.logical_and(band % NBANDS == b, jnp.logical_and(bins >= low, bins < high))
         select = jnp.where(inside, 1.0, select)
         count = jnp.full((NBANDS, LANES), high - low, jnp.int32).astype(F32)
         width_of = jnp.where(iota((NBANDS, LANES), 0) == b, count, width_of)
@@ -292,7 +298,7 @@
             inverse = stack(*[scale[i]] * STEP)
             source = stack(*[turn[i]] * STEP)
             means.append([
-                (up - jnp.take_along_axis(jnp.where(kept, up, down), source, axis=1)) * inverse
+                (up - jnp.take_along_axis(jnp.where(kept, up, down), source, axis=1, mode=lax.GatherScatterMode.PROMISE_IN_BOUNDS)) * inverse
                 for up, down in zip(ups, downs)
             ])
         for q in range(4):
@@ -301,11 +307,11 @@
                 at = pl.multiple_of(place[n] * 4 * LANES + q * LANES, LANES)
                 ratio_out[:, pl.ds(at, LANES)] = ratio[n * ROWS : (n + 1) * ROWS]
         total = dot(lanes(*split(power, 2)), sel[...])
+        total = jnp.where(iota((2 * rows, LANES), 1) // NBANDS == iota((2 * rows, LANES), 0) % ROWS, total, 0.0)
+        total = total.reshape(2 * STEP, ROWS, LANES).sum(axis=1)
         for n in range(STEP):
             for f in range(2):
-                at = pl.multiple_of((place[n] * 2 + f) * ROWS, ROWS)
-                begin = f * rows + n * ROWS
-                bands[pl.ds(at, ROWS), :] = total[begin : begin + ROWS]
+                bands[pl.ds(place[n] * 2 + f, 1), :] = total[f * STEP + n : f * STEP + n + 1]
 
     receive(0, 3)
     r[slabs] = r[0]
@@ -351,7 +357,7 @@
         functools.partial(kernel, slabs, groups),
         out_shape=(
             jax.ShapeDtypeStruct((ROWS, total), BF16),
-            jax.ShapeDtypeStruct((total // FRAME * ROWS, LANES), F32),
+            jax.ShapeDtypeStruct((total // FRAME, LANES), F32),
             jax.ShapeDtypeStruct((NBANDS, LANES), F32),
         ),
         in_specs=[hbm] * 7,
@@ -394,7 +400,7 @@
         ),
         in_specs=[vmem] * 3,
         out_specs=(hbm, hbm),
-        scratch_shapes=[pltpu.VMEM((ROWS, NBANDS, frames), F32), dma((2,))],
+        scratch_shapes=[pltpu.VMEM((ROWS, NBANDS, frames), F32), dma((5,))],
         compiler_params=pltpu.CompilerParams(vmem_limit_bytes=8 * 2**20),
     )(ratio, bands, widths)
 

time: 41.3 us -> 41.3 us (level)
  no operation moved by 1% of the time
where the time goes in v6:
time: 41.3 us; the launch traced here: 41.2 us
  Pallas kernels  40.5 us (98%)
  between operations  0.64 us (2%)
    pallas_call x1, Pallas kernels, body(): pl.pallas_call(functools.partial(kernel, slabs, groups), out_shape=(jax.S...  39.5 us
    pallas_call x1, Pallas kernels, body(): pl.pallas_call(finish, out_shape=(jax.ShapeDtypeStruct((1, ROWS, total),...  1.02 us

profile of v6, /device:TPU:33, one launch (start us, length us, event | category | flops | bytes accessed | tf_op | source)
XLA Modules:
  0.0 41.2 jit_solution(6936126329115499361)
XLA Ops:
  0.6 39.5 %shard_map.86 = (bf16[16,32768]{1,0:T(8,128)(2,1)S(1)}, f32[128,128]{1,0:T(8,128)S(1)}, f32[8,128]{1,0:T(8,128)S(1)}) custom-call(bf16[1024,512]{1,0:T(8,128)(2,1)} %traces.1, bf16[129]{0:T(256)(128)(2,1)} %taps_in.1, s32[8,128]{1,0:T(8,128)} %bitcast.1, s32[1024]{0:T(1024)} %sta_in.1, s32[1024]{0:T(1024)} %lta_in.1, s32[9]{0:T(128)} %edges_in.1, ...), custom_call_target="tpu_custom_call" | custom-call | flops 4000000000 | bytes 3145728 | tf_op jit(solution)/shard_map/pallas_call | solution.py:356
  40.2 1.0 %shard_map.87 = (bf16[1,16,32768]{2,1,0:T(8,128)(2,1)}, f32[1,16,8,128]{3,2,1,0:T(8,128)}) custom-call(bf16[16,32768]{1,0:T(8,128)(2,1)S(1)} %get-tuple-element.5.ratio, f32[128,128]{1,0:T(8,128)S(1)} %get-tuple-element.6.bands, f32[8,128]{1,0:T(8,128)S(1)} %get-tuple-element.7.widths), custom_call_target="tpu_custom_call" | custom-call | tf_op jit(solution)/shard_map/pallas_call | solution.py:395

commit v7 on v5

--- a/solution.py
+++ b/solution.py
@@ -137,12 +137,12 @@
 
     def to_hi():
         return pltpu.make_async_remote_copy(
-            src_ref=traces.at[pl.ds(chans - ROWS, ROWS)], dst_ref=lo_halo, send_sem=hsend.at[0],
+            src_ref=x.at[pl.ds(chans - ROWS, ROWS)], dst_ref=lo_halo, send_sem=hsend.at[0],
             recv_sem=hrecv.at[0], device_id=(me, g + 1), device_id_type=MESH)
 
     def to_lo():
         return pltpu.make_async_remote_copy(
-            src_ref=traces.at[pl.ds(0, ROWS)], dst_ref=hi_halo, send_sem=hsend.at[1],
+            src_ref=x.at[pl.ds(0, ROWS)], dst_ref=hi_halo, send_sem=hsend.at[1],
             recv_sem=hrecv.at[1], device_id=(me, g - 1), device_id_type=MESH)
 
     @pl.when(has_hi)

time: 41.3 us -> 41 us (level)
  no operation moved by 1% of the time
where the time goes in v7:
time: 41 us; the launch traced here: 40.9 us
  Pallas kernels  40.3 us (98%)
  between operations  0.64 us (2%)
    pallas_call x1, Pallas kernels, body(): pl.pallas_call(functools.partial(kernel, slabs, groups), out_shape=(jax.S...  39.3 us
    pallas_call x1, Pallas kernels, body(): pl.pallas_call(finish, out_shape=(jax.ShapeDtypeStruct((1, ROWS, total),...  1.03 us

profile of v7, /device:TPU:33, one launch (start us, length us, event | category | flops | bytes accessed | tf_op | source)
XLA Modules:
  0.0 40.9 jit_solution(1707296506039181798)
XLA Ops:
  0.6 39.3 %shard_map.86 = (bf16[16,32768]{1,0:T(8,128)(2,1)S(1)}, f32[2048,128]{1,0:T(8,128)S(1)}, f32[8,128]{1,0:T(8,128)S(1)}) custom-call(bf16[1024,512]{1,0:T(8,128)(2,1)} %traces.1, bf16[129]{0:T(256)(128)(2,1)} %taps_in.1, s32[8,128]{1,0:T(8,128)} %bitcast.1, s32[1024]{0:T(1024)} %sta_in.1, s32[1024]{0:T(1024)} %lta_in.1, s32[9]{0:T(128)} %edges_in.1, ...), custom_call_target="tpu_custom_call" | custom-call | flops 4000000000 | bytes 3145728 | tf_op jit(solution)/shard_map/pallas_call | solution.py:350
  39.9 1.0 %shard_map.87 = (bf16[1,16,32768]{2,1,0:T(8,128)(2,1)}, f32[1,16,8,128]{3,2,1,0:T(8,128)}) custom-call(bf16[16,32768]{1,0:T(8,128)(2,1)S(1)} %get-tuple-element.5.ratio, f32[2048,128]{1,0:T(8,128)S(1)} %get-tuple-element.6.bands, f32[8,128]{1,0:T(8,128)S(1)} %get-tuple-element.7.widths), custom_call_target="tpu_custom_call" | custom-call | tf_op jit(solution)/shard_map/pallas_call | solution.py:389
